TPU v7x, 32 devices: a whole 2x2x4 slice. The times are simulated.
32 devices in a mesh: grp: 2 (over y), seq: 8 (over z, core), sp: 2 (over x), rep: 1.
Axes of the slice: x: 2, y: 2, z: 4, core: 2. Of those that a mesh axis runs over, the one named last changes fastest.
Arguments:
- queries: bfloat16 [32, 192, 2048], P(('grp', 'sp', 'seq'), 'rep'), parts along dimension 0, may hold values from -8 to 8
- keys: bfloat16 [32, 192, 2048], P(('grp', 'sp', 'seq'), 'rep'), parts along dimension 0, may hold values from -6 to 6
- values: bfloat16 [32, 192, 2048], P(('grp', 'sp', 'seq'), 'rep'), parts along dimension 0, may hold values from -16 to 16
- text_keys: bfloat16 [512, 2048], P('grp'), parts along dimension 0, may hold values from -6 to 6
- text_values: bfloat16 [512, 2048], P('grp'), parts along dimension 0, may hold values from -16 to 16
- text_count: int32 [2], P('grp'), parts along dimension 0, may hold values from 128 to 256
Outputs:
- attended: bfloat16 [32, 192, 2048], P(('grp', 'sp', 'seq'), 'rep'), parts along dimension 0
There are 2 independent parts, one for each index of `grp`. A program takes and returns all parts, laid end to end along the dimension named above; each array names one. Nothing has to cross between parts.
All inputs are finite; a program needn't handle non-finite values.
Results may differ from a plain program's by a relative error of at most 0.0035.
Values may be sent and summed in bfloat16 or wider, within the bound.
No kernel may reach another device: no remote copies, remote signals or barrier semaphores. Data moves between devices by JAX's collectives and lax.ppermute only.
A program may use at most 64 MiB of HBM per device.

v0:
```python
import functools
import math

import jax
import jax.numpy as jnp
from jax import lax
from jax.experimental import pallas as pl
from jax.experimental.pallas import tpu as pltpu
from jax.sharding import PartitionSpec as P

HDIM = 128
COLS = 4

masked_score = -1e30
exp2_scale = math.log2(math.e) / math.sqrt(HDIM)
vmem_limit = 14 * 2**20
move_limit = 2 * 2**20


def pack_kernel(slots, at, *refs):
    n = len(refs) - len(slots) - 1
    sources, outs, sems = refs[:n], refs[n:-1], refs[-1]
    copies = []
    for (k, chosen), out in zip(slots, outs):
        width = out.shape[2]
        head = pl.multiple_of((at[0] ^ k) * width, width)
        for j, i in enumerate(chosen):
            source = sources[i].at[0, :, pl.ds(head, width)]
            copies.append(pltpu.make_async_copy(source, out.at[j], sems.at[len(copies)]))
    for copy in copies:
        copy.start()
    for copy in copies:
        copy.wait()


def pack(place, sources, width, slots):
    shapes = [(len(chosen), sources[chosen[0]].shape[1], width) for _, chosen in slots]
    return pl.pallas_call(
        functools.partial(pack_kernel, slots),
        in_specs=[pl.BlockSpec(memory_space=pltpu.SMEM)]
        + [pl.BlockSpec(memory_space=pltpu.HBM)] * len(sources),
        out_specs=[pl.BlockSpec(memory_space=pltpu.VMEM)] * len(slots),
        out_shape=[jax.ShapeDtypeStruct(shape, jnp.bfloat16) for shape in shapes],
        scratch_shapes=[pltpu.SemaphoreType.DMA((sum(shape[0] for shape in shapes),))],
        cost_estimate=pl.CostEstimate(
            flops=0, bytes_accessed=4 * sum(map(math.prod, shapes)), transcendentals=0
        ),
        compiler_params=pltpu.CompilerParams(vmem_limit_bytes=move_limit),
    )(place, *sources)


def join_kernel(tiles, *refs):
    at = 0
    for ref in refs[:-1]:
        if tiles:
            refs[-1][at] = ref[:2]
            at += 1
        else:
            refs[-1][at : at + ref.shape[0]] = ref[...]
            at += ref.shape[0]


def join(parts):
    tiles = parts[0].ndim == 3
    count = len(parts) if tiles else sum(part.shape[0] for part in parts)
    shape = (count, 2, *parts[0].shape[-2:])
    return pl.pallas_call(
        functools.partial(join_kernel, tiles),
        out_shape=jax.ShapeDtypeStruct(shape, jnp.bfloat16),
        cost_estimate=pl.CostEstimate(
            flops=0, bytes_accessed=4 * math.prod(shape), transcendentals=0
        ),
        compiler_params=pltpu.CompilerParams(vmem_limit_bytes=move_limit),
    )(*parts)


def attend_kernel(flag, turns, begin, info, *refs):
    n = 2 * len(turns)
    queries, (text, own, other, halo) = refs[:n], refs[n : n + 4]
    outs, (keys, vals) = refs[n + 4 : -2], refs[-2:]
    length, width = own.shape[2:]
    rows = queries[0].shape[1]
    text_len = text.shape[1]
    base = info[0]
    text_live = lax.broadcasted_iota(jnp.int32, (1, text_len), 1) < info[1]

    def run(turn, at_query, with_halo):
        q_refs, out_refs = queries[at_query : at_query + 2], outs[at_query : at_query + 2]
        pieces = [(own, 0), (own, 1), (other, 0), (other, 1), None]
        pieces += [(halo, 0), (halo, 1)] if with_halo else []
        cut = len(pieces)
        pieces += [(own, 2), (other, 2)] + ([(halo, 2)] if with_halo else [])
        ends = [0]
        for piece in pieces:
            at = slice(ends[-1], ends[-1] + (text_len if piece is None else length))
            for side, dst in enumerate((keys, vals)):
                if piece is None:
                    dst[at] = text[side]
                else:
                    dst[at] = piece[0][base ^ (piece[1] ^ turn), side]
            ends.append(at.stop)
        main, inner = ends[cut], slice(ends[cut], ends[-1])
        first, second = [ref[ref.shape[0] - 1] for ref in q_refs]
        q_outer = jnp.where(base == 0, first, second)
        q_inner = jnp.where(base == 0, second, first)
        q_both = jnp.concatenate([q_outer, q_inner], axis=0)

        def scores_of(q, span, head):
            return lax.dot_general(
                q[:, head],
                keys[span, head],
                (((1,), (1,)), ((), ())),
                preferred_element_type=jnp.float32,
            )

        heads = [slice(at, at + HDIM) for at in range(0, width, HDIM)]
        scores = [
            (scores_of(q_both, slice(0, main), head), scores_of(q_inner, inner, head))
            for head in heads
        ]
        for head, (s_main, s_inner) in zip(heads, scores):
            parts = [
                s_main[:, : ends[4]],
                jnp.where(text_live, s_main[:, ends[4] : ends[5]], masked_score),
            ]
            if with_halo:
                parts.append(s_main[:, ends[5] :])
            tops = [jnp.max(s, axis=-1, keepdims=True) for s in parts]
            top = functools.reduce(jnp.maximum, tops)
            top_inner = jnp.maximum(top[rows:], jnp.max(s_inner, axis=-1, keepdims=True))
            top = jnp.concatenate([top[:rows], top_inner], axis=0) * exp2_scale
            total, summed, at = 0.0, 0.0, 0
            for s in parts:
                w = jnp.exp2(s * exp2_scale - top)
                total = total + jnp.sum(w, axis=-1, keepdims=True)
                summed = summed + jnp.dot(
                    w.astype(jnp.bfloat16),
                    vals[at : at + s.shape[1], head],
                    preferred_element_type=jnp.float32,
                )
                at += s.shape[1]
            w = jnp.exp2(s_inner * exp2_scale - top[rows:])
            total_inner = total[rows:] + jnp.sum(w, axis=-1, keepdims=True)
            summed_inner = summed[rows:] + jnp.dot(
                w.astype(jnp.bfloat16), vals[inner, head], preferred_element_type=jnp.float32
            )
            if begin:
                for i, row in (
                    (at_query + base, (summed[:rows], top[:rows], total[:rows])),
                    (at_query + 1 - base, (summed_inner, top[rows:], total_inner)),
                ):
                    for out, x in zip(outs, row):
                        out[i, :, head] = jnp.broadcast_to(x, (rows, HDIM))
                continue
            o_outer = (summed[:rows] / total[:rows]).astype(jnp.bfloat16)
            o_inner = (summed_inner / total_inner).astype(jnp.bfloat16)
            out_refs[0][0, :, head] = jnp.where(base == 0, o_outer, o_inner)
            out_refs[1][0, :, head] = jnp.where(base == 0, o_inner, o_outer)

    def run_all(with_halo):
        for t, turn in enumerate(turns):
            run(turn, 2 * t, with_halo)

    if begin:
        run_all(False)
    else:
        pl.when(info[flag] == 1)(lambda: run_all(True))
        pl.when(info[flag] == 0)(lambda: run_all(False))


def finish_kernel(flag, turns, info, *refs):
    n = 2 * len(turns)
    queries, (halo, sums, tops, totals), outs = refs[:n], refs[n : n + 4], refs[n + 4 :]
    rows, width = sums.shape[1:]
    base = info[0]

    def run(with_halo):
        units = []
        for t, turn in enumerate(turns):
            first, second = [ref[ref.shape[0] - 1] for ref in queries[2 * t : 2 * t + 2]]
            q_inner = jnp.where(base == 0, second, first)
            q_both = jnp.concatenate([jnp.where(base == 0, first, second), q_inner], axis=0)
            slots = [base ^ (place ^ turn) for place in range(3)]
            for at in range(0, width, HDIM):
                head = slice(at, at + HDIM)
                scores = []
                for q, js in ((q_both, slots[:2]), (q_inner, slots[2:])) if with_halo else ():
                    key = jnp.concatenate([halo[j, 0, :, head] for j in js], axis=0)
                    scores.append(
                        lax.dot_general(
                            q[:, head],
                            key,
                            (((1,), (1,)), ((), ())),
                            preferred_element_type=jnp.float32,
                        )
                    )
                units.append((t, slots, head, scores))
        for t, slots, head, scores in units:
            outer, inner = 2 * t + base, 2 * t + 1 - base
            summed, old_top, total = [
                jnp.concatenate([ref[outer, :, head], ref[inner, :, head]], axis=0)
                for ref in (sums, tops, totals)
            ]
            if with_halo:
                s_pair, s_third = scores
                val, val_third = [
                    jnp.concatenate([halo[j, 1, :, head] for j in js], axis=0)
                    for js in (slots[:2], slots[2:])
                ]
                top = jnp.max(s_pair, axis=-1, keepdims=True)
                top_third = jnp.max(s_third, axis=-1, keepdims=True)
                top = jnp.concatenate([top[:rows], jnp.maximum(top[rows:], top_third)], axis=0)
                top = jnp.maximum(top * exp2_scale, old_top[:, :1])
                keep = jnp.exp2(old_top - top)
                w = jnp.exp2(s_pair * exp2_scale - top)
                w_third = jnp.exp2(s_third * exp2_scale - top[rows:])
                added, added_third = [
                    jnp.dot(x.astype(jnp.bfloat16), v, preferred_element_type=jnp.float32)
                    for x, v in ((w, val), (w_third, val_third))
                ]
                more = jnp.sum(w, axis=-1, keepdims=True)
                more_third = jnp.sum(w_third, axis=-1, keepdims=True)
                summed = summed * keep + jnp.concatenate(
                    [added[:rows], added[rows:] + added_third], axis=0
                )
                total = total * keep + jnp.concatenate(
                    [more[:rows], more[rows:] + more_third], axis=0
                )
            result = (summed / total).astype(jnp.bfloat16)
            o_outer, o_inner = result[:rows], result[rows:]
            outs[2 * t][0, :, head] = jnp.where(base == 0, o_outer, o_inner)
            outs[2 * t + 1][0, :, head] = jnp.where(base == 0, o_inner, o_outer)

    pl.when(info[flag] == 1)(lambda: run(True))
    pl.when(info[flag] == 0)(lambda: run(False))


def finish(info, flag, turns, queries, halo, began):
    _, rows, width = began[0].shape
    length = halo.shape[2]
    pairs = len(queries) * width // HDIM * rows * 3 * length
    return pl.pallas_call(
        functools.partial(finish_kernel, flag, turns),
        in_specs=[pl.BlockSpec(memory_space=pltpu.SMEM)]
        + [pl.BlockSpec(memory_space=pltpu.VMEM)] * (len(queries) + 4),
        out_shape=[jax.ShapeDtypeStruct((1, rows, width), jnp.bfloat16)] * len(queries),
        cost_estimate=pl.CostEstimate(
            flops=4 * pairs * HDIM,
            bytes_accessed=width * (4 * 3 * length + 16 * rows * len(queries)),
            transcendentals=pairs,
        ),
        compiler_params=pltpu.CompilerParams(vmem_limit_bytes=vmem_limit),
    )(info, *queries, halo, *began)


def attend(info, flag, turns, queries, text, own, other, halo=None):
    rows = queries[-1].shape[1]
    length, width = own.shape[2:]
    total_keys = 9 * length + text.shape[1]
    pairs = len(queries) * width // HDIM * rows * total_keys
    if halo is None:
        out_shape = [jax.ShapeDtypeStruct((len(queries), rows, width), jnp.float32)] * 3
    else:
        out_shape = [jax.ShapeDtypeStruct((1, rows, width), jnp.bfloat16)] * len(queries)
    begin, halo = halo is None, own if halo is None else halo
    return pl.pallas_call(
        functools.partial(attend_kernel, flag, turns, begin),
        in_specs=[pl.BlockSpec(memory_space=pltpu.SMEM)]
        + [pl.BlockSpec(memory_space=pltpu.VMEM)] * (len(queries) + 4),
        scratch_shapes=[pltpu.VMEM((total_keys, width), jnp.bfloat16)] * 2,
        out_shape=out_shape,
        cost_estimate=pl.CostEstimate(
            flops=4 * pairs * HDIM,
            bytes_accessed=width * 4 * (total_keys + rows * len(queries)),
            transcendentals=pairs,
        ),
        compiler_params=pltpu.CompilerParams(vmem_limit_bytes=vmem_limit),
    )(info, *queries, text, own, other, halo)


def spread_kernel(slots, place, *refs):
    out, sems = refs[-2:]
    width = refs[0].shape[2]
    copies = []
    for i, (k, ref) in enumerate(zip(slots, refs)):
        at = pl.multiple_of((place[0] ^ k) * width, width)
        copies.append(pltpu.make_async_copy(ref, out.at[:, :, pl.ds(at, width)], sems.at[i]))
    for copy in copies:
        copy.start()
    for copy in copies:
        copy.wait()


def spread(place, pieces, out_width, into=None):
    slots = sorted(pieces)
    shape = (*pieces[slots[0]].shape[:2], out_width)
    extra = [] if into is None else [into]
    return pl.pallas_call(
        functools.partial(spread_kernel, slots),
        in_specs=[pl.BlockSpec(memory_space=pltpu.SMEM)]
        + [pl.BlockSpec(memory_space=pltpu.VMEM)] * len(slots)
        + [pl.BlockSpec(memory_space=pl.ANY)] * len(extra),
        out_specs=pl.BlockSpec(memory_space=pl.ANY),
        out_shape=jax.ShapeDtypeStruct(shape, jnp.bfloat16),
        input_output_aliases={1 + len(slots): 0} if extra else {},
        scratch_shapes=[pltpu.SemaphoreType.DMA((len(slots),))],
        cost_estimate=pl.CostEstimate(
            flops=0, bytes_accessed=4 * math.prod(shape), transcendentals=0
        ),
        compiler_params=pltpu.CompilerParams(vmem_limit_bytes=move_limit),
    )(place, *[pieces[k] for k in slots], *extra)


def after(x, *others):
    return lax.optimization_barrier((x, *others))[0]


def body(queries, keys, values, text_keys, text_values, text_count):
    n_seq, n_sp = lax.axis_size("seq"), lax.axis_size("sp")
    tile = lax.axis_index("sp") * n_seq + lax.axis_index("seq")
    n_tiles, span = n_sp * n_seq, 2 * COLS
    col, odd, place, pair = tile % COLS, tile // COLS % 2, tile % span, tile // span
    n_pairs = n_tiles // span
    if lax.axis_size("rep") > 1:
        keys = lax.all_gather(keys, "rep", axis=1, tiled=True)
        values = lax.all_gather(values, "rep", axis=1, tiled=True)
    part = queries.shape[2] // span
    near_slots, far_slots = range(COLS), range(COLS, span)

    def send(x, k):
        return lax.ppermute(x, "seq", [(i, i ^ k) for i in range(n_seq)])

    def to_halo(x, down):
        pairs = [(i, i + span if i // COLS % 2 == down else i - span) for i in range(n_tiles)]
        flat = lambda i: i % n_seq * n_sp + i // n_seq
        pairs = [(flat(i), flat(j)) for i, j in pairs if 0 <= j < n_tiles]
        return lax.ppermute(x, ("seq", "sp"), pairs)

    low_halo, high_halo = pair > 0, pair < n_pairs - 1
    near_halo = jnp.where(odd == 1, low_halo, high_halo)
    far_halo = jnp.where(odd == 1, high_halo, low_halo)
    base = (col == 1) | (col == 2)
    entries = (base, text_count[0], near_halo, far_halo)
    info = jnp.stack([jnp.asarray(x, jnp.int32) for x in entries])

    block = place.reshape(1)
    sources = [keys, values, queries]
    kinds = [(0, 1, 2)] if queries.shape == keys.shape else [(0, 1), (2,)]

    sent = dict(zip(far_slots, pack(block, sources[:2], part, [(k, (0, 1)) for k in far_slots])))
    kv = {k: send(sent[k], k) for k in (4, 5)}
    inputs = [after(x, *sent.values()) for x in sources]
    wanted = [(k, kind) for k in near_slots for kind in kinds]
    near_sent = pack(block, inputs, part, wanted)
    near_sent = [near_sent[k * len(kinds) : (k + 1) * len(kinds)] for k in near_slots]
    near = [near_sent[0]] + [[send(x, k) for x in near_sent[k]] for k in (1, 2, 3)]
    inputs = [after(x, near[1][0]) for x in (queries, text_keys[None], text_values[None])]
    wanted = [(k, (0,)) for k in far_slots] + [(0, (1, 2))]
    q4, q5, q6, q7, text = pack(block, inputs, part, wanted)
    kv[6] = send(after(sent[6], near[1][0]), 6)
    kv[7] = send(after(sent[7], near[1][0], text), 7)
    kv.update({k: near[k][0] for k in near_slots})
    q = {k: near[k][-1] for k in near_slots}
    own = join([kv[k] for k in near_slots])
    own_halo = to_halo(after(own, kv[4], kv[5], kv[6]), 1)
    other = join([kv[k] for k in far_slots])
    other_halo = to_halo(other, 0)
    q4, q5 = after(q4, other), after(q5, other)
    q[4], q[5] = send(q4, 4), send(q5, 5)
    q[6], q[7] = send(after(q6, own_halo), 6), send(after(q7, own_halo), 7)
    o = {}
    pieces = [q[0], q[1], q[3], q[2]]
    began = attend(info, 3, [0, 3], pieces, text, own, other)
    x4, x5 = attend(info, 2, [0], [after(q[4], began[0]), q[5]], text, own, other, own_halo)
    o[4], o[5] = send(x4, 4), send(x5, 5)
    x7, x6 = attend(info, 2, [3], [after(q[7], x4), q[6]], text, own, other, own_halo)
    o[7], o[6] = send(x7, 7), send(x6, 6)
    other_halo = after(other_halo, x7, o[4])
    o[0], x1, x3, x2 = finish(info, 3, [0, 3], pieces, other_halo, began)
    o[3], o[2], o[1] = send(x3, 3), send(x2, 2), send(x1, 1)
    out = spread(block, {k: o[k] for k in far_slots}, queries.shape[2])
    return spread(block, {k: o[k] for k in near_slots}, queries.shape[2], into=out)


def solution(mesh):
    in_specs = (
        P(("grp", "sp", "seq"), "rep", None),
        P(("grp", "sp", "seq"), "rep", None),
        P(("grp", "sp", "seq"), "rep", None),
        P("grp", None),
        P("grp", None),
        P("grp"),
    )
    out_specs = P(("grp", "sp", "seq"), "rep", None)
    return jax.shard_map(body, mesh=mesh, in_specs=in_specs, out_specs=out_specs, check_vma=False)
```

profile of v0, /device:TPU:3, one launch (start us, length us, event | category | flops | bytes accessed | tf_op | source)
XLA Modules:
  0.0 91.4 jit_solution(13442998928416463332)
XLA Ops:
  0.0 1.1 %copy-done = bf16[1,192,2048]{2,1,0:T(8,128)(2,1)S(1)} copy-done((bf16[1,192,2048]{2,1,0:T(8,128)(2,1)S(1)}, bf16[1,192,2048]{2,1,0:T(8,128)(2,1)}, u32[]{:S(2)}) %copy-start) | copy-done | bytes 786456
  1.1 1.1 %copy-done.1 = bf16[1,192,2048]{2,1,0:T(8,128)(2,1)S(1)} copy-done((bf16[1,192,2048]{2,1,0:T(8,128)(2,1)S(1)}, bf16[1,192,2048]{2,1,0:T(8,128)(2,1)}, u32[]{:S(2)}) %copy-start.1) | copy-done | bytes 786456
  2.3 0.2 shard_map.64
  2.5 0.9 %copy-done.2 = bf16[1,192,2048]{2,1,0:T(8,128)(2,1)S(1)} copy-done((bf16[1,192,2048]{2,1,0:T(8,128)(2,1)S(1)}, bf16[1,192,2048]{2,1,0:T(8,128)(2,1)}, u32[]{:S(2)}) %copy-start.2) | copy-done | bytes 786456
  3.4 0.3 shard_map.65
  3.7 0.7 collective-permute-start
  4.5 1.3 %collective-permute-start.1 = (bf16[3,192,256]{2,1,0:T(8,128)(2,1)S(1)}, bf16[3,192,256]{2,1,0:T(8,128)(2,1)S(1)}, u32[]{:S(2)}, u32[]{:S(2)}) collective-permute-start(bf16[3,192,256]{2,1,0:T(8,128)(2,1)S(1)} %get-tuple-element.54), channel_id=1, source_target_pairs={{0,6},{2,4},{4,2},{6,0},{8,14},{10,12},{12,10},{14,8},{1,7},{3,5},... | collective-permute-start | bytes 884744 | tf_op jit(solution)/shard_map/ppermute | solution.py:331
  5.7 0.2 collective-permute-start.2
  5.9 2.3 %collective-permute-start.3 = (bf16[2,192,256]{2,1,0:T(8,128)(2,1)S(1)}, bf16[2,192,256]{2,1,0:T(8,128)(2,1)S(1)}, u32[]{:S(2)}, u32[]{:S(2)}) collective-permute-start(bf16[2,192,256]{2,1,0:T(8,128)(2,1)S(1)} %get-tuple-element.45), channel_id=1, source_target_pairs={{0,8},{2,10},{4,12},{6,14},{8,0},{10,2},{12,4},{14,6},{1,9},{3,11}... | collective-permute-start | bytes 589832 | tf_op jit(solution)/shard_map/ppermute | solution.py:331
  8.2 0.9 %collective-permute-start.4 = (bf16[2,192,256]{2,1,0:T(8,128)(2,1)S(1)}, bf16[2,192,256]{2,1,0:T(8,128)(2,1)S(1)}, u32[]{:S(2)}, u32[]{:S(2)}) collective-permute-start(bf16[2,192,256]{2,1,0:T(8,128)(2,1)S(1)} %get-tuple-element.46), channel_id=1, source_target_pairs={{0,10},{2,8},{4,14},{6,12},{8,2},{10,0},{12,6},{14,4},{1,11},{3,9}... | collective-permute-start | bytes 589832 | tf_op jit(solution)/shard_map/ppermute | solution.py:331
  9.1 0.0 collective-permute-done.refs_1_
  9.1 3.3 %collective-permute-start.5 = (bf16[2,192,256]{2,1,0:T(8,128)(2,1)S(1)}, bf16[2,192,256]{2,1,0:T(8,128)(2,1)S(1)}, u32[]{:S(2)}, u32[]{:S(2)}) collective-permute-start(bf16[2,192,256]{2,1,0:T(8,128)(2,1)S(1)} %get-tuple-element.56), channel_id=1, source_target_pairs={{0,12},{2,14},{4,8},{6,10},{8,4},{10,6},{12,0},{14,2},{1,13},{3,15... | collective-permute-start | bytes 589832 | tf_op jit(solution)/shard_map/ppermute | solution.py:331
  12.5 0.2 shard_map.66
  12.6 0.0 copy-start.5
  12.7 9.5 %collective-permute-done.1.refs_3_.refs_2_ = bf16[3,192,256]{2,1,0:T(8,128)(2,1)S(1)} collective-permute-done((bf16[3,192,256]{2,1,0:T(8,128)(2,1)S(1)}, bf16[3,192,256]{2,1,0:T(8,128)(2,1)S(1)}, u32[]{:S(2)}, u32[]{:S(2)}) %collective-permute-start.1) | collective-permute-done | bytes 294944 | tf_op jit(solution)/shard_map/ppermute | solution.py:331
  22.1 2.8 %collective-permute-start.6 = (bf16[2,192,256]{2,1,0:T(8,128)(2,1)S(1)}, bf16[2,192,256]{2,1,0:T(8,128)(2,1)S(1)}, u32[]{:S(2)}, u32[]{:S(2)}) collective-permute-start(bf16[2,192,256]{2,1,0:T(8,128)(2,1)S(1)} %get-tuple-element.61), channel_id=1, source_target_pairs={{0,14},{2,12},{4,10},{6,8},{8,6},{10,4},{12,2},{14,0},{1,15},{3,13... | collective-permute-start | bytes 589832 | tf_op jit(solution)/shard_map/ppermute | solution.py:331
  24.9 2.7 %collective-permute-done.2.refs_2_.refs_3_ = bf16[3,192,256]{2,1,0:T(8,128)(2,1)S(1)} collective-permute-done((bf16[3,192,256]{2,1,0:T(8,128)(2,1)S(1)}, bf16[3,192,256]{2,1,0:T(8,128)(2,1)S(1)}, u32[]{:S(2)}, u32[]{:S(2)}) %collective-permute-start.2) | collective-permute-done | bytes 294944 | tf_op jit(solution)/shard_map/ppermute | solution.py:331
  27.6 0.1 shard_map.68.refs_5_.refs_7_.refs_3_
  27.7 0.0 collective-permute-done.3.refs_0_
  27.8 6.2 %collective-permute-done.5.refs_2_ = bf16[2,192,256]{2,1,0:T(8,128)(2,1)S(1)} collective-permute-done((bf16[2,192,256]{2,1,0:T(8,128)(2,1)S(1)}, bf16[2,192,256]{2,1,0:T(8,128)(2,1)S(1)}, u32[]{:S(2)}, u32[]{:S(2)}) %collective-permute-start.5) | collective-permute-done | bytes 196640 | tf_op jit(solution)/shard_map/ppermute | solution.py:331
  33.9 3.0 %collective-permute-start.8 = (bf16[4,2,192,256]{3,2,1,0:T(8,128)(2,1)S(1)}, bf16[4,2,192,256]{3,2,1,0:T(8,128)(2,1)}, u32[]{:S(2)}, u32[]{:S(2)}) collective-permute-start(bf16[4,2,192,256]{3,2,1,0:T(8,128)(2,1)S(1)} %shard_map.68.refs_5_.refs_7_.refs_3_), channel_id=1, source_target_pairs={{8,9},{10,11},{12,13},{14,15},{1,0},{3,2},{5,4},{7,6},{24,25},{26,... | collective-permute-start | bytes 2359304 | tf_op jit(solution)/shard_map/ppermute | solution.py:337
  37.0 1.5 %collective-permute-done.6.refs_3_ = bf16[2,192,256]{2,1,0:T(8,128)(2,1)S(1)} collective-permute-done((bf16[2,192,256]{2,1,0:T(8,128)(2,1)S(1)}, bf16[2,192,256]{2,1,0:T(8,128)(2,1)S(1)}, u32[]{:S(2)}, u32[]{:S(2)}) %collective-permute-start.6) | collective-permute-done | bytes 196640 | tf_op jit(solution)/shard_map/ppermute | solution.py:331
  38.5 0.1 shard_map.67.refs_6_.refs_4_
  38.5 1.3 %collective-permute-start.7 = (bf16[4,2,192,256]{3,2,1,0:T(8,128)(2,1)S(1)}, bf16[4,2,192,256]{3,2,1,0:T(8,128)(2,1)S(1)}, u32[]{:S(2)}, u32[]{:S(2)}) collective-permute-start(bf16[4,2,192,256]{3,2,1,0:T(8,128)(2,1)S(1)} %shard_map.67.refs_6_.refs_4_), channel_id=1, source_target_pairs={{0,1},{2,3},{4,5},{6,7},{9,8},{11,10},{13,12},{15,14},{16,17},{18,... | collective-permute-start | bytes 2359304 | tf_op jit(solution)/shard_map/ppermute | solution.py:337
  40.5 0.1 pad_add_fusion.info
  40.6 7.8 %collective-permute-start.10 = (bf16[1,192,256]{2,1,0:T(8,128)(2,1)}, bf16[1,192,256]{2,1,0:T(8,128)(2,1)S(1)}, u32[]{:S(2)}, u32[]{:S(2)}) collective-permute-start(bf16[1,192,256]{2,1,0:T(8,128)(2,1)} %copy-done.12), channel_id=1, source_target_pairs={{0,8},{2,10},{4,12},{6,14},{8,0},{10,2},{12,4},{14,6},{1,9},{3,11}... | collective-permute-start | bytes 294920 | tf_op jit(solution)/shard_map/ppermute | solution.py:331
  48.4 2.2 %collective-permute-start.11 = (bf16[1,192,256]{2,1,0:T(8,128)(2,1)}, bf16[1,192,256]{2,1,0:T(8,128)(2,1)S(1)}, u32[]{:S(2)}, u32[]{:S(2)}) collective-permute-start(bf16[1,192,256]{2,1,0:T(8,128)(2,1)} %copy-done.11), channel_id=1, source_target_pairs={{0,10},{2,8},{4,14},{6,12},{8,2},{10,0},{12,6},{14,4},{1,11},{3,9}... | collective-permute-start | bytes 294920 | tf_op jit(solution)/shard_map/ppermute | solution.py:331
  50.6 0.9 %copy-done.6 = bf16[2,256,256]{2,1,0:T(8,128)(2,1)S(1)} copy-done((bf16[2,256,256]{2,1,0:T(8,128)(2,1)S(1)}, bf16[2,256,256]{2,1,0:T(8,128)(2,1)}, u32[]{:S(2)}) %copy-start.6) | copy-done | bytes 262168
  51.5 4.4 %shard_map.69 = (f32[4,192,256]{2,1,0:T(8,128)S(1)}, f32[4,192,256]{2,1,0:T(8,128)S(1)}, f32[4,192,256]{2,1,0:T(8,128)S(1)}) custom-call(s32[4]{0:T(128)S(1)} %pad_add_fusion.info, bf16[3,192,256]{2,1,0:T(8,128)(2,1)S(1)} %get-tuple-element.52.refs_0_, bf16[3,192,256]{2,1,0:T(8,128)(2,1)S(1)} %collective-permute-done.refs_1_, ...), custom_call_target="tpu_custom_call" | custom-call | flops 1560281088 | bytes 2818048 | tf_op jit(solution)/shard_map/pallas_call | solution.py:266
  55.9 0.0 collective-permute-done.8.refs_5_
  56.0 0.9 collective-permute-start.9
  56.9 2.6 %collective-permute-start.12 = (bf16[1,192,256]{2,1,0:T(8,128)(2,1)S(1)}, bf16[1,192,256]{2,1,0:T(8,128)(2,1)S(1)}, u32[]{:S(2)}, u32[]{:S(2)}) collective-permute-start(bf16[1,192,256]{2,1,0:T(8,128)(2,1)S(1)} %copy-done.8), channel_id=1, source_target_pairs={{0,12},{2,14},{4,8},{6,10},{8,4},{10,6},{12,0},{14,2},{1,13},{3,15... | collective-permute-start | bytes 294920 | tf_op jit(solution)/shard_map/ppermute | solution.py:331
  59.5 0.0 collective-permute-done.10.refs_0_
  59.5 3.0 %shard_map.70 = (bf16[1,192,256]{2,1,0:T(8,128)(2,1)S(1)}, bf16[1,192,256]{2,1,0:T(8,128)(2,1)S(1)}) custom-call(s32[4]{0:T(128)S(1)} %pad_add_fusion.info, bf16[1,192,256]{2,1,0:T(8,128)(2,1)S(1)} %collective-permute-done.10.refs_0_, bf16[1,192,256]{2,1,0:T(8,128)(2,1)S(1)} %collective-permute-done.11.refs_1_, bf16[2,256,256]{2,1,0:T(8,128)(2,1)S(1)} %copy-done.6, ...), custom_call_target="tpu_custom_call" | custom-call | flops 780140544 | bytes 2424832 | tf_op jit(solution)/shard_map/pallas_call | solution.py:266
  62.6 4.5 %collective-permute-start.13 = (bf16[1,192,256]{2,1,0:T(8,128)(2,1)S(1)}, bf16[1,192,256]{2,1,0:T(8,128)(2,1)S(1)}, u32[]{:S(2)}, u32[]{:S(2)}) collective-permute-start(bf16[1,192,256]{2,1,0:T(8,128)(2,1)S(1)} %get-tuple-element.71), channel_id=1, source_target_pairs={{0,8},{2,10},{4,12},{6,14},{8,0},{10,2},{12,4},{14,6},{1,9},{3,11}... | collective-permute-start | bytes 294920 | tf_op jit(solution)/shard_map/ppermute | solution.py:331
  67.1 0.0 collective-permute-start.17
  67.1 0.0 collective-permute-done.9.refs_0_
  67.1 3.2 %shard_map.71 = (bf16[1,192,256]{2,1,0:T(8,128)(2,1)S(1)}, bf16[1,192,256]{2,1,0:T(8,128)(2,1)S(1)}) custom-call(s32[4]{0:T(128)S(1)} %pad_add_fusion.info, bf16[1,192,256]{2,1,0:T(8,128)(2,1)S(1)} %collective-permute-done.9.refs_0_, bf16[1,192,256]{2,1,0:T(8,128)(2,1)S(1)} %collective-permute-done.12.refs_1_, bf16[2,256,256]{2,1,0:T(8,128)(2,1)S(1)} %copy-done.6, ...), custom_call_target="tpu_custom_call" | custom-call | flops 780140544 | bytes 2424832 | tf_op jit(solution)/shard_map/pallas_call | solution.py:266
  70.3 1.4 %collective-permute-start.18 = (bf16[1,192,256]{2,1,0:T(8,128)(2,1)S(1)}, bf16[1,192,256]{2,1,0:T(8,128)(2,1)S(1)}, u32[]{:S(2)}, u32[]{:S(2)}) collective-permute-start(bf16[1,192,256]{2,1,0:T(8,128)(2,1)S(1)} %get-tuple-element.84), channel_id=1, source_target_pairs={{0,12},{2,14},{4,8},{6,10},{8,4},{10,6},{12,0},{14,2},{1,13},{3,15... | collective-permute-start | bytes 294920 | tf_op jit(solution)/shard_map/ppermute | solution.py:331
  71.7 2.6 %collective-permute-start.19 = (bf16[1,192,256]{2,1,0:T(8,128)(2,1)S(1)}, bf16[1,192,256]{2,1,0:T(8,128)(2,1)S(1)}, u32[]{:S(2)}, u32[]{:S(2)}) collective-permute-start(bf16[1,192,256]{2,1,0:T(8,128)(2,1)S(1)} %get-tuple-element.75), channel_id=1, source_target_pairs={{0,14},{2,12},{4,10},{6,8},{8,6},{10,4},{12,2},{14,0},{1,15},{3,13... | collective-permute-start | bytes 294920 | tf_op jit(solution)/shard_map/ppermute | solution.py:331
  74.2 5.0 %collective-permute-done.13.refs_0_ = bf16[1,192,256]{2,1,0:T(8,128)(2,1)S(1)} collective-permute-done((bf16[1,192,256]{2,1,0:T(8,128)(2,1)S(1)}, bf16[1,192,256]{2,1,0:T(8,128)(2,1)S(1)}, u32[]{:S(2)}, u32[]{:S(2)}) %collective-permute-start.13) | collective-permute-done | bytes 98336 | tf_op jit(solution)/shard_map/ppermute | solution.py:331
  79.3 3.6 %shard_map.72 = (bf16[1,192,256]{2,1,0:T(8,128)(2,1)S(1)}, bf16[1,192,256]{2,1,0:T(8,128)(2,1)S(1)}, bf16[1,192,256]{2,1,0:T(8,128)(2,1)S(1)}, bf16[1,192,256]{2,1,0:T(8,128)(2,1)S(1)}) custom-call(s32[4]{0:T(128)S(1)} %pad_add_fusion.info, bf16[3,192,256]{2,1,0:T(8,128)(2,1)S(1)} %get-tuple-element.52.refs_0_, ...), custom_call_target="tpu_custom_call" | custom-call | flops 452984832 | bytes 3735552 | tf_op jit(solution)/shard_map/pallas_call | solution.py:242
  82.8 1.0 %collective-permute-start.14 = (bf16[1,192,256]{2,1,0:T(8,128)(2,1)S(1)}, bf16[1,192,256]{2,1,0:T(8,128)(2,1)S(1)}, u32[]{:S(2)}, u32[]{:S(2)}) collective-permute-start(bf16[1,192,256]{2,1,0:T(8,128)(2,1)S(1)} %get-tuple-element.80), channel_id=1, source_target_pairs={{0,2},{2,0},{4,6},{6,4},{8,10},{10,8},{12,14},{14,12},{1,3},{3,1},... | collective-permute-start | bytes 294920 | tf_op jit(solution)/shard_map/ppermute | solution.py:331
  83.8 1.7 %collective-permute-start.16 = (bf16[1,192,256]{2,1,0:T(8,128)(2,1)S(1)}, bf16[1,192,256]{2,1,0:T(8,128)(2,1)S(1)}, u32[]{:S(2)}, u32[]{:S(2)}) collective-permute-start(bf16[1,192,256]{2,1,0:T(8,128)(2,1)S(1)} %get-tuple-element.82), channel_id=1, source_target_pairs={{0,6},{2,4},{4,2},{6,0},{8,14},{10,12},{12,10},{14,8},{1,7},{3,5},... | collective-permute-start | bytes 294920 | tf_op jit(solution)/shard_map/ppermute | solution.py:331
  85.5 0.8 shard_map.73.refs_4_
  86.3 1.9 %collective-permute-done.15.refs_2_ = bf16[1,192,256]{2,1,0:T(8,128)(2,1)S(1)} collective-permute-done((bf16[1,192,256]{2,1,0:T(8,128)(2,1)S(1)}, bf16[1,192,256]{2,1,0:T(8,128)(2,1)S(1)}, u32[]{:S(2)}, u32[]{:S(2)}) %collective-permute-start.15) | collective-permute-done | bytes 98336 | tf_op jit(solution)/shard_map/ppermute | solution.py:331
  88.2 2.3 %collective-permute-done.16.refs_3_ = bf16[1,192,256]{2,1,0:T(8,128)(2,1)S(1)} collective-permute-done((bf16[1,192,256]{2,1,0:T(8,128)(2,1)S(1)}, bf16[1,192,256]{2,1,0:T(8,128)(2,1)S(1)}, u32[]{:S(2)}, u32[]{:S(2)}) %collective-permute-start.16) | collective-permute-done | bytes 98336 | tf_op jit(solution)/shard_map/ppermute | solution.py:331
  90.5 0.8 shard_map.74
  (30 shorter events, 0.1 us)
Async XLA Ops:
  0.0 1.1 %copy-start = (bf16[1,192,2048]{2,1,0:T(8,128)(2,1)S(1)}, bf16[1,192,2048]{2,1,0:T(8,128)(2,1)}, u32[]{:S(2)}) copy-start(bf16[1,192,2048]{2,1,0:T(8,128)(2,1)} %refs_0_.2) | copy-start | bytes 2359300
  1.1 1.1 %copy-start.1 = (bf16[1,192,2048]{2,1,0:T(8,128)(2,1)S(1)}, bf16[1,192,2048]{2,1,0:T(8,128)(2,1)}, u32[]{:S(2)}) copy-start(bf16[1,192,2048]{2,1,0:T(8,128)(2,1)} %refs_1_.2) | copy-start | bytes 2359300
  2.3 1.1 %copy-start.2 = (bf16[1,192,2048]{2,1,0:T(8,128)(2,1)S(1)}, bf16[1,192,2048]{2,1,0:T(8,128)(2,1)}, u32[]{:S(2)}) copy-start(bf16[1,192,2048]{2,1,0:T(8,128)(2,1)} %refs_0_.3) | copy-start | bytes 2359300
  3.4 9.1 %copy-start.3 = (bf16[256,2048]{1,0:T(8,128)(2,1)S(1)}, bf16[256,2048]{1,0:T(8,128)(2,1)}, u32[]{:S(2)}) copy-start(bf16[256,2048]{1,0:T(8,128)(2,1)} %param.9) | copy-start | bytes 3145732
  3.4 9.1 %copy-start.4 = (bf16[256,2048]{1,0:T(8,128)(2,1)S(1)}, bf16[256,2048]{1,0:T(8,128)(2,1)}, u32[]{:S(2)}) copy-start(bf16[256,2048]{1,0:T(8,128)(2,1)} %param.10) | copy-start | bytes 3145732
  3.7 5.4 %collective-permute-start = (bf16[3,192,256]{2,1,0:T(8,128)(2,1)S(1)}, bf16[3,192,256]{2,1,0:T(8,128)(2,1)S(1)}, u32[]{:S(2)}, u32[]{:S(2)}) collective-permute-start(bf16[3,192,256]{2,1,0:T(8,128)(2,1)S(1)} %get-tuple-element.53), channel_id=1, source_target_pairs={{0,2},{2,0},{4,6},{6,4},{8,10},{10,8},{12,14},{14,12},{1,3},{3,1},... | collective-permute-start | bytes 884744 | tf_op jit(solution)/shard_map/ppermute | solution.py:331
  4.5 17.7 %collective-permute-start.1 = (bf16[3,192,256]{2,1,0:T(8,128)(2,1)S(1)}, bf16[3,192,256]{2,1,0:T(8,128)(2,1)S(1)}, u32[]{:S(2)}, u32[]{:S(2)}) collective-permute-start(bf16[3,192,256]{2,1,0:T(8,128)(2,1)S(1)} %get-tuple-element.54), channel_id=1, source_target_pairs={{0,6},{2,4},{4,2},{6,0},{8,14},{10,12},{12,10},{14,8},{1,7},{3,5},... | collective-permute-start | bytes 884744 | tf_op jit(solution)/shard_map/ppermute | solution.py:331
  5.7 21.9 %collective-permute-start.2 = (bf16[3,192,256]{2,1,0:T(8,128)(2,1)S(1)}, bf16[3,192,256]{2,1,0:T(8,128)(2,1)S(1)}, u32[]{:S(2)}, u32[]{:S(2)}) collective-permute-start(bf16[3,192,256]{2,1,0:T(8,128)(2,1)S(1)} %get-tuple-element.55), channel_id=1, source_target_pairs={{0,4},{2,6},{4,0},{6,2},{8,12},{10,14},{12,8},{14,10},{1,5},{3,7},... | collective-permute-start | bytes 884744 | tf_op jit(solution)/shard_map/ppermute | solution.py:331
  5.9 21.8 %collective-permute-start.3 = (bf16[2,192,256]{2,1,0:T(8,128)(2,1)S(1)}, bf16[2,192,256]{2,1,0:T(8,128)(2,1)S(1)}, u32[]{:S(2)}, u32[]{:S(2)}) collective-permute-start(bf16[2,192,256]{2,1,0:T(8,128)(2,1)S(1)} %get-tuple-element.45), channel_id=1, source_target_pairs={{0,8},{2,10},{4,12},{6,14},{8,0},{10,2},{12,4},{14,6},{1,9},{3,11}... | collective-permute-start | bytes 589832 | tf_op jit(solution)/shard_map/ppermute | solution.py:331
  8.2 19.5 %collective-permute-start.4 = (bf16[2,192,256]{2,1,0:T(8,128)(2,1)S(1)}, bf16[2,192,256]{2,1,0:T(8,128)(2,1)S(1)}, u32[]{:S(2)}, u32[]{:S(2)}) collective-permute-start(bf16[2,192,256]{2,1,0:T(8,128)(2,1)S(1)} %get-tuple-element.46), channel_id=1, source_target_pairs={{0,10},{2,8},{4,14},{6,12},{8,2},{10,0},{12,6},{14,4},{1,11},{3,9}... | collective-permute-start | bytes 589832 | tf_op jit(solution)/shard_map/ppermute | solution.py:331
  9.1 24.8 %collective-permute-start.5 = (bf16[2,192,256]{2,1,0:T(8,128)(2,1)S(1)}, bf16[2,192,256]{2,1,0:T(8,128)(2,1)S(1)}, u32[]{:S(2)}, u32[]{:S(2)}) collective-permute-start(bf16[2,192,256]{2,1,0:T(8,128)(2,1)S(1)} %get-tuple-element.56), channel_id=1, source_target_pairs={{0,12},{2,14},{4,8},{6,10},{8,4},{10,6},{12,0},{14,2},{1,13},{3,15... | collective-permute-start | bytes 589832 | tf_op jit(solution)/shard_map/ppermute | solution.py:331
  12.6 15.0 %copy-start.5 = (bf16[2,256,256]{2,1,0:T(8,128)(2,1)}, bf16[2,256,256]{2,1,0:T(8,128)(2,1)S(1)}, u32[]{:S(2)}) copy-start(bf16[2,256,256]{2,1,0:T(8,128)(2,1)S(1)} %get-tuple-element.60.refs_4_.refs_2_) | copy-start | bytes 786436
  12.7 15.0 %copy-start.7 = (bf16[1,192,256]{2,1,0:T(8,128)(2,1)}, bf16[1,192,256]{2,1,0:T(8,128)(2,1)S(1)}, u32[]{:S(2)}) copy-start(bf16[1,192,256]{2,1,0:T(8,128)(2,1)S(1)} %get-tuple-element.74) | copy-start | bytes 294916
  12.7 15.0 %copy-start.9 = (bf16[1,192,256]{2,1,0:T(8,128)(2,1)}, bf16[1,192,256]{2,1,0:T(8,128)(2,1)S(1)}, u32[]{:S(2)}) copy-start(bf16[1,192,256]{2,1,0:T(8,128)(2,1)S(1)} %get-tuple-element.64) | copy-start | bytes 294916
  12.7 15.0 %copy-start.11 = (bf16[1,192,256]{2,1,0:T(8,128)(2,1)}, bf16[1,192,256]{2,1,0:T(8,128)(2,1)S(1)}, u32[]{:S(2)}) copy-start(bf16[1,192,256]{2,1,0:T(8,128)(2,1)S(1)} %get-tuple-element.70) | copy-start | bytes 294916
  12.7 15.0 %copy-start.12 = (bf16[1,192,256]{2,1,0:T(8,128)(2,1)}, bf16[1,192,256]{2,1,0:T(8,128)(2,1)S(1)}, u32[]{:S(2)}) copy-start(bf16[1,192,256]{2,1,0:T(8,128)(2,1)S(1)} %get-tuple-element.66) | copy-start | bytes 294916
  22.1 16.3 %collective-permute-start.6 = (bf16[2,192,256]{2,1,0:T(8,128)(2,1)S(1)}, bf16[2,192,256]{2,1,0:T(8,128)(2,1)S(1)}, u32[]{:S(2)}, u32[]{:S(2)}) collective-permute-start(bf16[2,192,256]{2,1,0:T(8,128)(2,1)S(1)} %get-tuple-element.61), channel_id=1, source_target_pairs={{0,14},{2,12},{4,10},{6,8},{8,6},{10,4},{12,2},{14,0},{1,15},{3,13... | collective-permute-start | bytes 589832 | tf_op jit(solution)/shard_map/ppermute | solution.py:331
  33.9 22.0 %collective-permute-start.8 = (bf16[4,2,192,256]{3,2,1,0:T(8,128)(2,1)S(1)}, bf16[4,2,192,256]{3,2,1,0:T(8,128)(2,1)}, u32[]{:S(2)}, u32[]{:S(2)}) collective-permute-start(bf16[4,2,192,256]{3,2,1,0:T(8,128)(2,1)S(1)} %shard_map.68.refs_5_.refs_7_.refs_3_), channel_id=1, source_target_pairs={{8,9},{10,11},{12,13},{14,15},{1,0},{3,2},{5,4},{7,6},{24,25},{26,... | collective-permute-start | bytes 2359304 | tf_op jit(solution)/shard_map/ppermute | solution.py:337
  38.5 35.7 %collective-permute-start.7 = (bf16[4,2,192,256]{3,2,1,0:T(8,128)(2,1)S(1)}, bf16[4,2,192,256]{3,2,1,0:T(8,128)(2,1)S(1)}, u32[]{:S(2)}, u32[]{:S(2)}) collective-permute-start(bf16[4,2,192,256]{3,2,1,0:T(8,128)(2,1)S(1)} %shard_map.67.refs_6_.refs_4_), channel_id=1, source_target_pairs={{0,1},{2,3},{4,5},{6,7},{9,8},{11,10},{13,12},{15,14},{16,17},{18,... | collective-permute-start | bytes 2359304 | tf_op jit(solution)/shard_map/ppermute | solution.py:337
  40.6 18.9 %collective-permute-start.10 = (bf16[1,192,256]{2,1,0:T(8,128)(2,1)}, bf16[1,192,256]{2,1,0:T(8,128)(2,1)S(1)}, u32[]{:S(2)}, u32[]{:S(2)}) collective-permute-start(bf16[1,192,256]{2,1,0:T(8,128)(2,1)} %copy-done.12), channel_id=1, source_target_pairs={{0,8},{2,10},{4,12},{6,14},{8,0},{10,2},{12,4},{14,6},{1,9},{3,11}... | collective-permute-start | bytes 294920 | tf_op jit(solution)/shard_map/ppermute | solution.py:331
  48.4 11.1 %collective-permute-start.11 = (bf16[1,192,256]{2,1,0:T(8,128)(2,1)}, bf16[1,192,256]{2,1,0:T(8,128)(2,1)S(1)}, u32[]{:S(2)}, u32[]{:S(2)}) collective-permute-start(bf16[1,192,256]{2,1,0:T(8,128)(2,1)} %copy-done.11), channel_id=1, source_target_pairs={{0,10},{2,8},{4,14},{6,12},{8,2},{10,0},{12,6},{14,4},{1,11},{3,9}... | collective-permute-start | bytes 294920 | tf_op jit(solution)/shard_map/ppermute | solution.py:331
  50.6 0.9 %copy-start.6 = (bf16[2,256,256]{2,1,0:T(8,128)(2,1)S(1)}, bf16[2,256,256]{2,1,0:T(8,128)(2,1)}, u32[]{:S(2)}) copy-start(bf16[2,256,256]{2,1,0:T(8,128)(2,1)} %copy-done.5) | copy-start | bytes 786436
  51.5 4.4 %copy-start.10 = (bf16[1,192,256]{2,1,0:T(8,128)(2,1)S(1)}, bf16[1,192,256]{2,1,0:T(8,128)(2,1)}, u32[]{:S(2)}) copy-start(bf16[1,192,256]{2,1,0:T(8,128)(2,1)} %copy-done.9) | copy-start | bytes 294916
  51.5 5.3 %copy-start.8 = (bf16[1,192,256]{2,1,0:T(8,128)(2,1)S(1)}, bf16[1,192,256]{2,1,0:T(8,128)(2,1)}, u32[]{:S(2)}) copy-start(bf16[1,192,256]{2,1,0:T(8,128)(2,1)} %copy-done.7) | copy-start | bytes 294916
  56.0 11.1 %collective-permute-start.9 = (bf16[1,192,256]{2,1,0:T(8,128)(2,1)S(1)}, bf16[1,192,256]{2,1,0:T(8,128)(2,1)S(1)}, u32[]{:S(2)}, u32[]{:S(2)}) collective-permute-start(bf16[1,192,256]{2,1,0:T(8,128)(2,1)S(1)} %copy-done.10), channel_id=1, source_target_pairs={{0,14},{2,12},{4,10},{6,8},{8,6},{10,4},{12,2},{14,0},{1,15},{3,13... | collective-permute-start | bytes 294920 | tf_op jit(solution)/shard_map/ppermute | solution.py:331
  56.9 10.2 %collective-permute-start.12 = (bf16[1,192,256]{2,1,0:T(8,128)(2,1)S(1)}, bf16[1,192,256]{2,1,0:T(8,128)(2,1)S(1)}, u32[]{:S(2)}, u32[]{:S(2)}) collective-permute-start(bf16[1,192,256]{2,1,0:T(8,128)(2,1)S(1)} %copy-done.8), channel_id=1, source_target_pairs={{0,12},{2,14},{4,8},{6,10},{8,4},{10,6},{12,0},{14,2},{1,13},{3,15... | collective-permute-start | bytes 294920 | tf_op jit(solution)/shard_map/ppermute | solution.py:331
  62.6 16.7 %collective-permute-start.13 = (bf16[1,192,256]{2,1,0:T(8,128)(2,1)S(1)}, bf16[1,192,256]{2,1,0:T(8,128)(2,1)S(1)}, u32[]{:S(2)}, u32[]{:S(2)}) collective-permute-start(bf16[1,192,256]{2,1,0:T(8,128)(2,1)S(1)} %get-tuple-element.71), channel_id=1, source_target_pairs={{0,8},{2,10},{4,12},{6,14},{8,0},{10,2},{12,4},{14,6},{1,9},{3,11}... | collective-permute-start | bytes 294920 | tf_op jit(solution)/shard_map/ppermute | solution.py:331
  67.1 16.8 %collective-permute-start.17 = (bf16[1,192,256]{2,1,0:T(8,128)(2,1)S(1)}, bf16[1,192,256]{2,1,0:T(8,128)(2,1)S(1)}, u32[]{:S(2)}, u32[]{:S(2)}) collective-permute-start(bf16[1,192,256]{2,1,0:T(8,128)(2,1)S(1)} %get-tuple-element.83), channel_id=1, source_target_pairs={{0,10},{2,8},{4,14},{6,12},{8,2},{10,0},{12,6},{14,4},{1,11},{3,9}... | collective-permute-start | bytes 294920 | tf_op jit(solution)/shard_map/ppermute | solution.py:331
  70.3 15.2 %collective-permute-start.18 = (bf16[1,192,256]{2,1,0:T(8,128)(2,1)S(1)}, bf16[1,192,256]{2,1,0:T(8,128)(2,1)S(1)}, u32[]{:S(2)}, u32[]{:S(2)}) collective-permute-start(bf16[1,192,256]{2,1,0:T(8,128)(2,1)S(1)} %get-tuple-element.84), channel_id=1, source_target_pairs={{0,12},{2,14},{4,8},{6,10},{8,4},{10,6},{12,0},{14,2},{1,13},{3,15... | collective-permute-start | bytes 294920 | tf_op jit(solution)/shard_map/ppermute | solution.py:331
  71.7 13.8 %collective-permute-start.19 = (bf16[1,192,256]{2,1,0:T(8,128)(2,1)S(1)}, bf16[1,192,256]{2,1,0:T(8,128)(2,1)S(1)}, u32[]{:S(2)}, u32[]{:S(2)}) collective-permute-start(bf16[1,192,256]{2,1,0:T(8,128)(2,1)S(1)} %get-tuple-element.75), channel_id=1, source_target_pairs={{0,14},{2,12},{4,10},{6,8},{8,6},{10,4},{12,2},{14,0},{1,15},{3,13... | collective-permute-start | bytes 294920 | tf_op jit(solution)/shard_map/ppermute | solution.py:331
  82.8 3.5 %collective-permute-start.14 = (bf16[1,192,256]{2,1,0:T(8,128)(2,1)S(1)}, bf16[1,192,256]{2,1,0:T(8,128)(2,1)S(1)}, u32[]{:S(2)}, u32[]{:S(2)}) collective-permute-start(bf16[1,192,256]{2,1,0:T(8,128)(2,1)S(1)} %get-tuple-element.80), channel_id=1, source_target_pairs={{0,2},{2,0},{4,6},{6,4},{8,10},{10,8},{12,14},{14,12},{1,3},{3,1},... | collective-permute-start | bytes 294920 | tf_op jit(solution)/shard_map/ppermute | solution.py:331
  83.8 4.4 %collective-permute-start.15 = (bf16[1,192,256]{2,1,0:T(8,128)(2,1)S(1)}, bf16[1,192,256]{2,1,0:T(8,128)(2,1)S(1)}, u32[]{:S(2)}, u32[]{:S(2)}) collective-permute-start(bf16[1,192,256]{2,1,0:T(8,128)(2,1)S(1)} %get-tuple-element.81), channel_id=1, source_target_pairs={{0,4},{2,6},{4,0},{6,2},{8,12},{10,14},{12,8},{14,10},{1,5},{3,7},... | collective-permute-start | bytes 294920 | tf_op jit(solution)/shard_map/ppermute | solution.py:331
  83.8 6.6 %collective-permute-start.16 = (bf16[1,192,256]{2,1,0:T(8,128)(2,1)S(1)}, bf16[1,192,256]{2,1,0:T(8,128)(2,1)S(1)}, u32[]{:S(2)}, u32[]{:S(2)}) collective-permute-start(bf16[1,192,256]{2,1,0:T(8,128)(2,1)S(1)} %get-tuple-element.82), channel_id=1, source_target_pairs={{0,6},{2,4},{4,2},{6,0},{8,14},{10,12},{12,10},{14,8},{1,7},{3,5},... | collective-permute-start | bytes 294920 | tf_op jit(solution)/shard_map/ppermute | solution.py:331
where the time goes:
time: 91.8 us; the launch traced here: 91.4 us
  starting transfers between devices  40.5 us (44%)
  waiting for transfers between devices  29 us (32%)
  Pallas kernels  16.5 us (18%)
  local copies, waits for them, and re-layouts  4.18 us (5%)
  between operations  1.09 us (1%)
    ppermute x18, starting transfers between devices, send(): return lax.ppermute(x, 'seq', [(i, i ^ k) for i in range(n_seq)])  36.2 us
    ppermute x18, waiting for transfers between devices, send(): return lax.ppermute(x, 'seq', [(i, i ^ k) for i in range(n_seq)])  29 us
    pallas_call x3, Pallas kernels, attend(): pl.pallas_call(functools.partial(attend_kernel, flag, turns, begin), in_s...  10.6 us
    ppermute x2, starting transfers between devices, to_halo(): return lax.ppermute(x, ('seq', 'sp'), pairs)  4.33 us
    unnamed x26, local copies, waits for them, and re-layouts  4.18 us
    pallas_call x1, Pallas kernels, finish(): pl.pallas_call(functools.partial(finish_kernel, flag, turns), in_specs=[p...  3.55 us
  transfers between devices with their start and end apart: 20, of which 7 were waited for; matrix products, arithmetic and copies ran while one was open for 0% of the time, Pallas kernels for 17%

commit v1 on v0

--- a/solution.py
+++ b/solution.py
@@ -367,7 +367,7 @@
     other_halo = to_halo(other, 0)
     q4, q5 = after(q4, other), after(q5, other)
     q[4], q[5] = send(q4, 4), send(q5, 5)
-    q[6], q[7] = send(after(q6, own_halo), 6), send(after(q7, own_halo), 7)
+    q[6], q[7] = send(after(q6, own_halo), 6), send(after(q7, other), 7)
     o = {}
     pieces = [q[0], q[1], q[3], q[2]]
     began = attend(info, 3, [0, 3], pieces, text, own, other)

time: 91.8 us -> 86.6 us (0.943)
  the two profiles are of different devices: /device:TPU:3 before, /device:TPU:0 now
where the time goes in v1:
time: 86.6 us; the launch traced here: 85.2 us
  starting transfers between devices  36.7 us (42%)
  waiting for transfers between devices  28.8 us (33%)
  Pallas kernels  14.3 us (17%)
  local copies, waits for them, and re-layouts  4.18 us (5%)
  between operations  1.1 us (1%)
    ppermute x18, starting transfers between devices, send(): return lax.ppermute(x, 'seq', [(i, i ^ k) for i in range(n_seq)])  31.8 us
    ppermute x18, waiting for transfers between devices, send(): return lax.ppermute(x, 'seq', [(i, i ^ k) for i in range(n_seq)])  28.8 us
    pallas_call x3, Pallas kernels, attend(): pl.pallas_call(functools.partial(attend_kernel, flag, turns, begin), in_s...  11.3 us
    ppermute x2, starting transfers between devices, to_halo(): return lax.ppermute(x, ('seq', 'sp'), pairs)  4.98 us
    unnamed x24, local copies, waits for them, and re-layouts  4.18 us
  transfers between devices with their start and end apart: 20, of which 8 were waited for; matrix products, arithmetic and copies ran while one was open for 0% of the time, Pallas kernels for 15%

profile of v1, /device:TPU:0, one launch (start us, length us, event | category | flops | bytes accessed | tf_op | source)
XLA Modules:
  0.0 85.2 jit_solution(6210968751238096114)
XLA Ops:
  0.0 1.1 %copy-done = bf16[1,192,2048]{2,1,0:T(8,128)(2,1)S(1)} copy-done((bf16[1,192,2048]{2,1,0:T(8,128)(2,1)S(1)}, bf16[1,192,2048]{2,1,0:T(8,128)(2,1)}, u32[]{:S(2)}) %copy-start) | copy-done | bytes 786456
  1.1 1.1 %copy-done.1 = bf16[1,192,2048]{2,1,0:T(8,128)(2,1)S(1)} copy-done((bf16[1,192,2048]{2,1,0:T(8,128)(2,1)S(1)}, bf16[1,192,2048]{2,1,0:T(8,128)(2,1)}, u32[]{:S(2)}) %copy-start.1) | copy-done | bytes 786456
  2.3 0.2 shard_map.64
  2.5 0.9 %copy-done.2 = bf16[1,192,2048]{2,1,0:T(8,128)(2,1)S(1)} copy-done((bf16[1,192,2048]{2,1,0:T(8,128)(2,1)S(1)}, bf16[1,192,2048]{2,1,0:T(8,128)(2,1)}, u32[]{:S(2)}) %copy-start.2) | copy-done | bytes 786456
  3.4 0.3 shard_map.65
  3.7 0.5 collective-permute-start
  4.2 2.7 %collective-permute-start.1 = (bf16[3,192,256]{2,1,0:T(8,128)(2,1)S(1)}, bf16[3,192,256]{2,1,0:T(8,128)(2,1)S(1)}, u32[]{:S(2)}, u32[]{:S(2)}) collective-permute-start(bf16[3,192,256]{2,1,0:T(8,128)(2,1)S(1)} %get-tuple-element.54), channel_id=1, source_target_pairs={{0,6},{2,4},{4,2},{6,0},{8,14},{10,12},{12,10},{14,8},{1,7},{3,5},... | collective-permute-start | bytes 884744 | tf_op jit(solution)/shard_map/ppermute | solution.py:331
  6.9 0.0 collective-permute-start.2
  7.0 3.0 %collective-permute-start.3 = (bf16[2,192,256]{2,1,0:T(8,128)(2,1)S(1)}, bf16[2,192,256]{2,1,0:T(8,128)(2,1)S(1)}, u32[]{:S(2)}, u32[]{:S(2)}) collective-permute-start(bf16[2,192,256]{2,1,0:T(8,128)(2,1)S(1)} %get-tuple-element.45), channel_id=1, source_target_pairs={{0,8},{2,10},{4,12},{6,14},{8,0},{10,2},{12,4},{14,6},{1,9},{3,11}... | collective-permute-start | bytes 589832 | tf_op jit(solution)/shard_map/ppermute | solution.py:331
  10.0 0.0 collective-permute-start.4
  10.0 0.0 collective-permute-done.refs_1_
  10.0 3.0 %collective-permute-start.5 = (bf16[2,192,256]{2,1,0:T(8,128)(2,1)S(1)}, bf16[2,192,256]{2,1,0:T(8,128)(2,1)S(1)}, u32[]{:S(2)}, u32[]{:S(2)}) collective-permute-start(bf16[2,192,256]{2,1,0:T(8,128)(2,1)S(1)} %get-tuple-element.56), channel_id=1, source_target_pairs={{0,12},{2,14},{4,8},{6,10},{8,4},{10,6},{12,0},{14,2},{1,13},{3,15... | collective-permute-start | bytes 589832 | tf_op jit(solution)/shard_map/ppermute | solution.py:331
  13.0 0.2 shard_map.66
  13.2 0.0 copy-start.5
  13.2 9.4 %collective-permute-done.1.refs_3_.refs_2_ = bf16[3,192,256]{2,1,0:T(8,128)(2,1)S(1)} collective-permute-done((bf16[3,192,256]{2,1,0:T(8,128)(2,1)S(1)}, bf16[3,192,256]{2,1,0:T(8,128)(2,1)S(1)}, u32[]{:S(2)}, u32[]{:S(2)}) %collective-permute-start.1) | collective-permute-done | bytes 294944 | tf_op jit(solution)/shard_map/ppermute | solution.py:331
  22.6 4.0 %collective-permute-start.6 = (bf16[2,192,256]{2,1,0:T(8,128)(2,1)S(1)}, bf16[2,192,256]{2,1,0:T(8,128)(2,1)S(1)}, u32[]{:S(2)}, u32[]{:S(2)}) collective-permute-start(bf16[2,192,256]{2,1,0:T(8,128)(2,1)S(1)} %get-tuple-element.61), channel_id=1, source_target_pairs={{0,14},{2,12},{4,10},{6,8},{8,6},{10,4},{12,2},{14,0},{1,15},{3,13... | collective-permute-start | bytes 589832 | tf_op jit(solution)/shard_map/ppermute | solution.py:331
  26.6 2.6 %collective-permute-done.2.refs_2_.refs_3_ = bf16[3,192,256]{2,1,0:T(8,128)(2,1)S(1)} collective-permute-done((bf16[3,192,256]{2,1,0:T(8,128)(2,1)S(1)}, bf16[3,192,256]{2,1,0:T(8,128)(2,1)S(1)}, u32[]{:S(2)}, u32[]{:S(2)}) %collective-permute-start.2) | collective-permute-done | bytes 294944 | tf_op jit(solution)/shard_map/ppermute | solution.py:331
  29.2 0.1 shard_map.68.refs_5_.refs_7_.refs_3_
  29.3 0.0 collective-permute-done.3.refs_0_
  29.4 6.9 %collective-permute-done.5.refs_2_ = bf16[2,192,256]{2,1,0:T(8,128)(2,1)S(1)} collective-permute-done((bf16[2,192,256]{2,1,0:T(8,128)(2,1)S(1)}, bf16[2,192,256]{2,1,0:T(8,128)(2,1)S(1)}, u32[]{:S(2)}, u32[]{:S(2)}) %collective-permute-start.5) | collective-permute-done | bytes 196640 | tf_op jit(solution)/shard_map/ppermute | solution.py:331
  36.3 1.3 %collective-permute-start.11 = (bf16[4,2,192,256]{3,2,1,0:T(8,128)(2,1)S(1)}, bf16[4,2,192,256]{3,2,1,0:T(8,128)(2,1)}, u32[]{:S(2)}, u32[]{:S(2)}) collective-permute-start(bf16[4,2,192,256]{3,2,1,0:T(8,128)(2,1)S(1)} %shard_map.68.refs_5_.refs_7_.refs_3_), channel_id=1, source_target_pairs={{8,9},{10,11},{12,13},{14,15},{1,0},{3,2},{5,4},{7,6},{24,25},{26,... | collective-permute-start | bytes 2359304 | tf_op jit(solution)/shard_map/ppermute | solution.py:337
  37.6 1.8 %collective-permute-done.6.refs_3_ = bf16[2,192,256]{2,1,0:T(8,128)(2,1)S(1)} collective-permute-done((bf16[2,192,256]{2,1,0:T(8,128)(2,1)S(1)}, bf16[2,192,256]{2,1,0:T(8,128)(2,1)S(1)}, u32[]{:S(2)}, u32[]{:S(2)}) %collective-permute-start.6) | collective-permute-done | bytes 196640 | tf_op jit(solution)/shard_map/ppermute | solution.py:331
  39.3 0.1 shard_map.67.refs_6_.refs_4_
  39.4 3.7 %collective-permute-start.7 = (bf16[4,2,192,256]{3,2,1,0:T(8,128)(2,1)S(1)}, bf16[4,2,192,256]{3,2,1,0:T(8,128)(2,1)S(1)}, u32[]{:S(2)}, u32[]{:S(2)}) collective-permute-start(bf16[4,2,192,256]{3,2,1,0:T(8,128)(2,1)S(1)} %shard_map.67.refs_6_.refs_4_), channel_id=1, source_target_pairs={{0,1},{2,3},{4,5},{6,7},{9,8},{11,10},{13,12},{15,14},{16,17},{18,... | collective-permute-start | bytes 2359304 | tf_op jit(solution)/shard_map/ppermute | solution.py:337
  43.8 0.1 pad_add_fusion.info
  43.9 4.8 %collective-permute-start.10 = (bf16[1,192,256]{2,1,0:T(8,128)(2,1)}, bf16[1,192,256]{2,1,0:T(8,128)(2,1)S(1)}, u32[]{:S(2)}, u32[]{:S(2)}) collective-permute-start(bf16[1,192,256]{2,1,0:T(8,128)(2,1)} %copy-done.10), channel_id=1, source_target_pairs={{0,10},{2,8},{4,14},{6,12},{8,2},{10,0},{12,6},{14,4},{1,11},{3,9}... | collective-permute-start | bytes 294920 | tf_op jit(solution)/shard_map/ppermute | solution.py:331
  48.7 1.9 %collective-permute-start.9 = (bf16[1,192,256]{2,1,0:T(8,128)(2,1)}, bf16[1,192,256]{2,1,0:T(8,128)(2,1)S(1)}, u32[]{:S(2)}, u32[]{:S(2)}) collective-permute-start(bf16[1,192,256]{2,1,0:T(8,128)(2,1)} %copy-done.11), channel_id=1, source_target_pairs={{0,8},{2,10},{4,12},{6,14},{8,0},{10,2},{12,4},{14,6},{1,9},{3,11}... | collective-permute-start | bytes 294920 | tf_op jit(solution)/shard_map/ppermute | solution.py:331
  50.6 1.3 %collective-permute-start.8 = (bf16[1,192,256]{2,1,0:T(8,128)(2,1)}, bf16[1,192,256]{2,1,0:T(8,128)(2,1)S(1)}, u32[]{:S(2)}, u32[]{:S(2)}) collective-permute-start(bf16[1,192,256]{2,1,0:T(8,128)(2,1)} %copy-done.9), channel_id=1, source_target_pairs={{0,14},{2,12},{4,10},{6,8},{8,6},{10,4},{12,2},{14,0},{1,15},{3,13... | collective-permute-start | bytes 294920 | tf_op jit(solution)/shard_map/ppermute | solution.py:331
  51.9 0.9 %copy-done.6 = bf16[2,256,256]{2,1,0:T(8,128)(2,1)S(1)} copy-done((bf16[2,256,256]{2,1,0:T(8,128)(2,1)S(1)}, bf16[2,256,256]{2,1,0:T(8,128)(2,1)}, u32[]{:S(2)}) %copy-start.6) | copy-done | bytes 262168
  52.8 4.4 %shard_map.69 = (f32[4,192,256]{2,1,0:T(8,128)S(1)}, f32[4,192,256]{2,1,0:T(8,128)S(1)}, f32[4,192,256]{2,1,0:T(8,128)S(1)}) custom-call(s32[4]{0:T(128)S(1)} %pad_add_fusion.info, bf16[3,192,256]{2,1,0:T(8,128)(2,1)S(1)} %get-tuple-element.52.refs_0_, bf16[3,192,256]{2,1,0:T(8,128)(2,1)S(1)} %collective-permute-done.refs_1_, ...), custom_call_target="tpu_custom_call" | custom-call | flops 1560281088 | bytes 2818048 | tf_op jit(solution)/shard_map/pallas_call | solution.py:266
  57.2 0.0 collective-permute-done.11.refs_5_
  57.2 2.2 %collective-permute-start.12 = (bf16[1,192,256]{2,1,0:T(8,128)(2,1)S(1)}, bf16[1,192,256]{2,1,0:T(8,128)(2,1)S(1)}, u32[]{:S(2)}, u32[]{:S(2)}) collective-permute-start(bf16[1,192,256]{2,1,0:T(8,128)(2,1)S(1)} %copy-done.8), channel_id=1, source_target_pairs={{0,12},{2,14},{4,8},{6,10},{8,4},{10,6},{12,0},{14,2},{1,13},{3,15... | collective-permute-start | bytes 294920 | tf_op jit(solution)/shard_map/ppermute | solution.py:331
  59.5 2.8 %collective-permute-done.9.refs_0_ = bf16[1,192,256]{2,1,0:T(8,128)(2,1)S(1)} collective-permute-done((bf16[1,192,256]{2,1,0:T(8,128)(2,1)}, bf16[1,192,256]{2,1,0:T(8,128)(2,1)S(1)}, u32[]{:S(2)}, u32[]{:S(2)}) %collective-permute-start.9) | collective-permute-done | bytes 98336 | tf_op jit(solution)/shard_map/ppermute | solution.py:331
  62.3 3.4 %shard_map.70 = (bf16[1,192,256]{2,1,0:T(8,128)(2,1)S(1)}, bf16[1,192,256]{2,1,0:T(8,128)(2,1)S(1)}) custom-call(s32[4]{0:T(128)S(1)} %pad_add_fusion.info, bf16[1,192,256]{2,1,0:T(8,128)(2,1)S(1)} %collective-permute-done.9.refs_0_, bf16[1,192,256]{2,1,0:T(8,128)(2,1)S(1)} %collective-permute-done.10.refs_1_, bf16[2,256,256]{2,1,0:T(8,128)(2,1)S(1)} %copy-done.6, ...), custom_call_target="tpu_custom_call" | custom-call | flops 780140544 | bytes 2424832 | tf_op jit(solution)/shard_map/pallas_call | solution.py:266
  65.7 0.3 collective-permute-start.13
  66.0 1.0 %collective-permute-start.17 = (bf16[1,192,256]{2,1,0:T(8,128)(2,1)S(1)}, bf16[1,192,256]{2,1,0:T(8,128)(2,1)S(1)}, u32[]{:S(2)}, u32[]{:S(2)}) collective-permute-start(bf16[1,192,256]{2,1,0:T(8,128)(2,1)S(1)} %get-tuple-element.83), channel_id=1, source_target_pairs={{0,10},{2,8},{4,14},{6,12},{8,2},{10,0},{12,6},{14,4},{1,11},{3,9}... | collective-permute-start | bytes 294920 | tf_op jit(solution)/shard_map/ppermute | solution.py:331
  67.0 3.6 %shard_map.71 = (bf16[1,192,256]{2,1,0:T(8,128)(2,1)S(1)}, bf16[1,192,256]{2,1,0:T(8,128)(2,1)S(1)}) custom-call(s32[4]{0:T(128)S(1)} %pad_add_fusion.info, bf16[1,192,256]{2,1,0:T(8,128)(2,1)S(1)} %collective-permute-done.8.refs_0_, bf16[1,192,256]{2,1,0:T(8,128)(2,1)S(1)} %collective-permute-done.12.refs_1_, bf16[2,256,256]{2,1,0:T(8,128)(2,1)S(1)} %copy-done.6, ...), custom_call_target="tpu_custom_call" | custom-call | flops 780140544 | bytes 2424832 | tf_op jit(solution)/shard_map/pallas_call | solution.py:266
  70.6 1.5 %collective-permute-start.18 = (bf16[1,192,256]{2,1,0:T(8,128)(2,1)S(1)}, bf16[1,192,256]{2,1,0:T(8,128)(2,1)S(1)}, u32[]{:S(2)}, u32[]{:S(2)}) collective-permute-start(bf16[1,192,256]{2,1,0:T(8,128)(2,1)S(1)} %get-tuple-element.84), channel_id=1, source_target_pairs={{0,12},{2,14},{4,8},{6,10},{8,4},{10,6},{12,0},{14,2},{1,13},{3,15... | collective-permute-start | bytes 294920 | tf_op jit(solution)/shard_map/ppermute | solution.py:331
  72.1 3.4 %collective-permute-start.19 = (bf16[1,192,256]{2,1,0:T(8,128)(2,1)S(1)}, bf16[1,192,256]{2,1,0:T(8,128)(2,1)S(1)}, u32[]{:S(2)}, u32[]{:S(2)}) collective-permute-start(bf16[1,192,256]{2,1,0:T(8,128)(2,1)S(1)} %get-tuple-element.75), channel_id=1, source_target_pairs={{0,14},{2,12},{4,10},{6,8},{8,6},{10,4},{12,2},{14,0},{1,15},{3,13... | collective-permute-start | bytes 294920 | tf_op jit(solution)/shard_map/ppermute | solution.py:331
  75.6 0.7 shard_map.72
  76.2 0.1 collective-permute-start.14
  76.3 0.4 collective-permute-start.15
  76.7 1.5 %collective-permute-start.16 = (bf16[1,192,256]{2,1,0:T(8,128)(2,1)S(1)}, bf16[1,192,256]{2,1,0:T(8,128)(2,1)S(1)}, u32[]{:S(2)}, u32[]{:S(2)}) collective-permute-start(bf16[1,192,256]{2,1,0:T(8,128)(2,1)S(1)} %get-tuple-element.82), channel_id=1, source_target_pairs={{0,6},{2,4},{4,2},{6,0},{8,14},{10,12},{12,10},{14,8},{1,7},{3,5},... | collective-permute-start | bytes 294920 | tf_op jit(solution)/shard_map/ppermute | solution.py:331
  78.2 2.2 %collective-permute-done.19.refs_3_ = bf16[1,192,256]{2,1,0:T(8,128)(2,1)S(1)} collective-permute-done((bf16[1,192,256]{2,1,0:T(8,128)(2,1)S(1)}, bf16[1,192,256]{2,1,0:T(8,128)(2,1)S(1)}, u32[]{:S(2)}, u32[]{:S(2)}) %collective-permute-start.19) | collective-permute-done | bytes 98336 | tf_op jit(solution)/shard_map/ppermute | solution.py:331
  80.4 0.8 shard_map.73.refs_4_
  81.2 2.0 %collective-permute-done.15.refs_2_ = bf16[1,192,256]{2,1,0:T(8,128)(2,1)S(1)} collective-permute-done((bf16[1,192,256]{2,1,0:T(8,128)(2,1)S(1)}, bf16[1,192,256]{2,1,0:T(8,128)(2,1)S(1)}, u32[]{:S(2)}, u32[]{:S(2)}) %collective-permute-start.15) | collective-permute-done | bytes 98336 | tf_op jit(solution)/shard_map/ppermute | solution.py:331
  83.2 1.0 %collective-permute-done.16.refs_3_ = bf16[1,192,256]{2,1,0:T(8,128)(2,1)S(1)} collective-permute-done((bf16[1,192,256]{2,1,0:T(8,128)(2,1)S(1)}, bf16[1,192,256]{2,1,0:T(8,128)(2,1)S(1)}, u32[]{:S(2)}, u32[]{:S(2)}) %collective-permute-start.16) | collective-permute-done | bytes 98336 | tf_op jit(solution)/shard_map/ppermute | solution.py:331
  84.2 0.8 shard_map.74
  (28 shorter events, 0.1 us)
Async XLA Ops:
  0.0 1.1 %copy-start = (bf16[1,192,2048]{2,1,0:T(8,128)(2,1)S(1)}, bf16[1,192,2048]{2,1,0:T(8,128)(2,1)}, u32[]{:S(2)}) copy-start(bf16[1,192,2048]{2,1,0:T(8,128)(2,1)} %refs_0_.2) | copy-start | bytes 2359300
  1.1 1.1 %copy-start.1 = (bf16[1,192,2048]{2,1,0:T(8,128)(2,1)S(1)}, bf16[1,192,2048]{2,1,0:T(8,128)(2,1)}, u32[]{:S(2)}) copy-start(bf16[1,192,2048]{2,1,0:T(8,128)(2,1)} %refs_1_.2) | copy-start | bytes 2359300
  2.3 1.1 %copy-start.2 = (bf16[1,192,2048]{2,1,0:T(8,128)(2,1)S(1)}, bf16[1,192,2048]{2,1,0:T(8,128)(2,1)}, u32[]{:S(2)}) copy-start(bf16[1,192,2048]{2,1,0:T(8,128)(2,1)} %refs_0_.3) | copy-start | bytes 2359300
  3.4 9.6 %copy-start.3 = (bf16[256,2048]{1,0:T(8,128)(2,1)S(1)}, bf16[256,2048]{1,0:T(8,128)(2,1)}, u32[]{:S(2)}) copy-start(bf16[256,2048]{1,0:T(8,128)(2,1)} %param.9) | copy-start | bytes 3145732
  3.4 9.6 %copy-start.4 = (bf16[256,2048]{1,0:T(8,128)(2,1)S(1)}, bf16[256,2048]{1,0:T(8,128)(2,1)}, u32[]{:S(2)}) copy-start(bf16[256,2048]{1,0:T(8,128)(2,1)} %param.10) | copy-start | bytes 3145732
  3.7 6.3 %collective-permute-start = (bf16[3,192,256]{2,1,0:T(8,128)(2,1)S(1)}, bf16[3,192,256]{2,1,0:T(8,128)(2,1)S(1)}, u32[]{:S(2)}, u32[]{:S(2)}) collective-permute-start(bf16[3,192,256]{2,1,0:T(8,128)(2,1)S(1)} %get-tuple-element.53), channel_id=1, source_target_pairs={{0,2},{2,0},{4,6},{6,4},{8,10},{10,8},{12,14},{14,12},{1,3},{3,1},... | collective-permute-start | bytes 884744 | tf_op jit(solution)/shard_map/ppermute | solution.py:331
  4.2 18.4 %collective-permute-start.1 = (bf16[3,192,256]{2,1,0:T(8,128)(2,1)S(1)}, bf16[3,192,256]{2,1,0:T(8,128)(2,1)S(1)}, u32[]{:S(2)}, u32[]{:S(2)}) collective-permute-start(bf16[3,192,256]{2,1,0:T(8,128)(2,1)S(1)} %get-tuple-element.54), channel_id=1, source_target_pairs={{0,6},{2,4},{4,2},{6,0},{8,14},{10,12},{12,10},{14,8},{1,7},{3,5},... | collective-permute-start | bytes 884744 | tf_op jit(solution)/shard_map/ppermute | solution.py:331
  6.9 22.3 %collective-permute-start.2 = (bf16[3,192,256]{2,1,0:T(8,128)(2,1)S(1)}, bf16[3,192,256]{2,1,0:T(8,128)(2,1)S(1)}, u32[]{:S(2)}, u32[]{:S(2)}) collective-permute-start(bf16[3,192,256]{2,1,0:T(8,128)(2,1)S(1)} %get-tuple-element.55), channel_id=1, source_target_pairs={{0,4},{2,6},{4,0},{6,2},{8,12},{10,14},{12,8},{14,10},{1,5},{3,7},... | collective-permute-start | bytes 884744 | tf_op jit(solution)/shard_map/ppermute | solution.py:331
  7.0 22.4 %collective-permute-start.3 = (bf16[2,192,256]{2,1,0:T(8,128)(2,1)S(1)}, bf16[2,192,256]{2,1,0:T(8,128)(2,1)S(1)}, u32[]{:S(2)}, u32[]{:S(2)}) collective-permute-start(bf16[2,192,256]{2,1,0:T(8,128)(2,1)S(1)} %get-tuple-element.45), channel_id=1, source_target_pairs={{0,8},{2,10},{4,12},{6,14},{8,0},{10,2},{12,4},{14,6},{1,9},{3,11}... | collective-permute-start | bytes 589832 | tf_op jit(solution)/shard_map/ppermute | solution.py:331
  10.0 19.4 %collective-permute-start.4 = (bf16[2,192,256]{2,1,0:T(8,128)(2,1)S(1)}, bf16[2,192,256]{2,1,0:T(8,128)(2,1)S(1)}, u32[]{:S(2)}, u32[]{:S(2)}) collective-permute-start(bf16[2,192,256]{2,1,0:T(8,128)(2,1)S(1)} %get-tuple-element.46), channel_id=1, source_target_pairs={{0,10},{2,8},{4,14},{6,12},{8,2},{10,0},{12,6},{14,4},{1,11},{3,9}... | collective-permute-start | bytes 589832 | tf_op jit(solution)/shard_map/ppermute | solution.py:331
  10.0 26.3 %collective-permute-start.5 = (bf16[2,192,256]{2,1,0:T(8,128)(2,1)S(1)}, bf16[2,192,256]{2,1,0:T(8,128)(2,1)S(1)}, u32[]{:S(2)}, u32[]{:S(2)}) collective-permute-start(bf16[2,192,256]{2,1,0:T(8,128)(2,1)S(1)} %get-tuple-element.56), channel_id=1, source_target_pairs={{0,12},{2,14},{4,8},{6,10},{8,4},{10,6},{12,0},{14,2},{1,13},{3,15... | collective-permute-start | bytes 589832 | tf_op jit(solution)/shard_map/ppermute | solution.py:331
  13.2 16.1 %copy-start.5 = (bf16[2,256,256]{2,1,0:T(8,128)(2,1)}, bf16[2,256,256]{2,1,0:T(8,128)(2,1)S(1)}, u32[]{:S(2)}) copy-start(bf16[2,256,256]{2,1,0:T(8,128)(2,1)S(1)} %get-tuple-element.60.refs_4_.refs_2_) | copy-start | bytes 786436
  13.2 16.1 %copy-start.7 = (bf16[1,192,256]{2,1,0:T(8,128)(2,1)}, bf16[1,192,256]{2,1,0:T(8,128)(2,1)S(1)}, u32[]{:S(2)}) copy-start(bf16[1,192,256]{2,1,0:T(8,128)(2,1)S(1)} %get-tuple-element.74) | copy-start | bytes 294916
  13.2 16.1 %copy-start.9 = (bf16[1,192,256]{2,1,0:T(8,128)(2,1)}, bf16[1,192,256]{2,1,0:T(8,128)(2,1)S(1)}, u32[]{:S(2)}) copy-start(bf16[1,192,256]{2,1,0:T(8,128)(2,1)S(1)} %get-tuple-element.63) | copy-start | bytes 294916
  13.2 16.1 %copy-start.10 = (bf16[1,192,256]{2,1,0:T(8,128)(2,1)}, bf16[1,192,256]{2,1,0:T(8,128)(2,1)S(1)}, u32[]{:S(2)}) copy-start(bf16[1,192,256]{2,1,0:T(8,128)(2,1)S(1)} %get-tuple-element.69) | copy-start | bytes 294916
  13.2 16.1 %copy-start.11 = (bf16[1,192,256]{2,1,0:T(8,128)(2,1)}, bf16[1,192,256]{2,1,0:T(8,128)(2,1)S(1)}, u32[]{:S(2)}) copy-start(bf16[1,192,256]{2,1,0:T(8,128)(2,1)S(1)} %get-tuple-element.65) | copy-start | bytes 294916
  22.6 16.7 %collective-permute-start.6 = (bf16[2,192,256]{2,1,0:T(8,128)(2,1)S(1)}, bf16[2,192,256]{2,1,0:T(8,128)(2,1)S(1)}, u32[]{:S(2)}, u32[]{:S(2)}) collective-permute-start(bf16[2,192,256]{2,1,0:T(8,128)(2,1)S(1)} %get-tuple-element.61), channel_id=1, source_target_pairs={{0,14},{2,12},{4,10},{6,8},{8,6},{10,4},{12,2},{14,0},{1,15},{3,13... | collective-permute-start | bytes 589832 | tf_op jit(solution)/shard_map/ppermute | solution.py:331
  36.3 20.9 %collective-permute-start.11 = (bf16[4,2,192,256]{3,2,1,0:T(8,128)(2,1)S(1)}, bf16[4,2,192,256]{3,2,1,0:T(8,128)(2,1)}, u32[]{:S(2)}, u32[]{:S(2)}) collective-permute-start(bf16[4,2,192,256]{3,2,1,0:T(8,128)(2,1)S(1)} %shard_map.68.refs_5_.refs_7_.refs_3_), channel_id=1, source_target_pairs={{8,9},{10,11},{12,13},{14,15},{1,0},{3,2},{5,4},{7,6},{24,25},{26,... | collective-permute-start | bytes 2359304 | tf_op jit(solution)/shard_map/ppermute | solution.py:337
  39.4 36.2 %collective-permute-start.7 = (bf16[4,2,192,256]{3,2,1,0:T(8,128)(2,1)S(1)}, bf16[4,2,192,256]{3,2,1,0:T(8,128)(2,1)S(1)}, u32[]{:S(2)}, u32[]{:S(2)}) collective-permute-start(bf16[4,2,192,256]{3,2,1,0:T(8,128)(2,1)S(1)} %shard_map.67.refs_6_.refs_4_), channel_id=1, source_target_pairs={{0,1},{2,3},{4,5},{6,7},{9,8},{11,10},{13,12},{15,14},{16,17},{18,... | collective-permute-start | bytes 2359304 | tf_op jit(solution)/shard_map/ppermute | solution.py:337
  43.9 18.4 %collective-permute-start.10 = (bf16[1,192,256]{2,1,0:T(8,128)(2,1)}, bf16[1,192,256]{2,1,0:T(8,128)(2,1)S(1)}, u32[]{:S(2)}, u32[]{:S(2)}) collective-permute-start(bf16[1,192,256]{2,1,0:T(8,128)(2,1)} %copy-done.10), channel_id=1, source_target_pairs={{0,10},{2,8},{4,14},{6,12},{8,2},{10,0},{12,6},{14,4},{1,11},{3,9}... | collective-permute-start | bytes 294920 | tf_op jit(solution)/shard_map/ppermute | solution.py:331
  48.7 13.6 %collective-permute-start.9 = (bf16[1,192,256]{2,1,0:T(8,128)(2,1)}, bf16[1,192,256]{2,1,0:T(8,128)(2,1)S(1)}, u32[]{:S(2)}, u32[]{:S(2)}) collective-permute-start(bf16[1,192,256]{2,1,0:T(8,128)(2,1)} %copy-done.11), channel_id=1, source_target_pairs={{0,8},{2,10},{4,12},{6,14},{8,0},{10,2},{12,4},{14,6},{1,9},{3,11}... | collective-permute-start | bytes 294920 | tf_op jit(solution)/shard_map/ppermute | solution.py:331
  50.6 15.4 %collective-permute-start.8 = (bf16[1,192,256]{2,1,0:T(8,128)(2,1)}, bf16[1,192,256]{2,1,0:T(8,128)(2,1)S(1)}, u32[]{:S(2)}, u32[]{:S(2)}) collective-permute-start(bf16[1,192,256]{2,1,0:T(8,128)(2,1)} %copy-done.9), channel_id=1, source_target_pairs={{0,14},{2,12},{4,10},{6,8},{8,6},{10,4},{12,2},{14,0},{1,15},{3,13... | collective-permute-start | bytes 294920 | tf_op jit(solution)/shard_map/ppermute | solution.py:331
  51.9 0.9 %copy-start.6 = (bf16[2,256,256]{2,1,0:T(8,128)(2,1)S(1)}, bf16[2,256,256]{2,1,0:T(8,128)(2,1)}, u32[]{:S(2)}) copy-start(bf16[2,256,256]{2,1,0:T(8,128)(2,1)} %copy-done.5) | copy-start | bytes 786436
  52.8 4.4 %copy-start.8 = (bf16[1,192,256]{2,1,0:T(8,128)(2,1)S(1)}, bf16[1,192,256]{2,1,0:T(8,128)(2,1)}, u32[]{:S(2)}) copy-start(bf16[1,192,256]{2,1,0:T(8,128)(2,1)} %copy-done.7) | copy-start | bytes 294916
  57.2 9.8 %collective-permute-start.12 = (bf16[1,192,256]{2,1,0:T(8,128)(2,1)S(1)}, bf16[1,192,256]{2,1,0:T(8,128)(2,1)S(1)}, u32[]{:S(2)}, u32[]{:S(2)}) collective-permute-start(bf16[1,192,256]{2,1,0:T(8,128)(2,1)S(1)} %copy-done.8), channel_id=1, source_target_pairs={{0,12},{2,14},{4,8},{6,10},{8,4},{10,6},{12,0},{14,2},{1,13},{3,15... | collective-permute-start | bytes 294920 | tf_op jit(solution)/shard_map/ppermute | solution.py:331
  65.7 9.9 %collective-permute-start.13 = (bf16[1,192,256]{2,1,0:T(8,128)(2,1)S(1)}, bf16[1,192,256]{2,1,0:T(8,128)(2,1)S(1)}, u32[]{:S(2)}, u32[]{:S(2)}) collective-permute-start(bf16[1,192,256]{2,1,0:T(8,128)(2,1)S(1)} %get-tuple-element.71), channel_id=1, source_target_pairs={{0,8},{2,10},{4,12},{6,14},{8,0},{10,2},{12,4},{14,6},{1,9},{3,11}... | collective-permute-start | bytes 294920 | tf_op jit(solution)/shard_map/ppermute | solution.py:331
  66.0 10.8 %collective-permute-start.17 = (bf16[1,192,256]{2,1,0:T(8,128)(2,1)S(1)}, bf16[1,192,256]{2,1,0:T(8,128)(2,1)S(1)}, u32[]{:S(2)}, u32[]{:S(2)}) collective-permute-start(bf16[1,192,256]{2,1,0:T(8,128)(2,1)S(1)} %get-tuple-element.83), channel_id=1, source_target_pairs={{0,10},{2,8},{4,14},{6,12},{8,2},{10,0},{12,6},{14,4},{1,11},{3,9}... | collective-permute-start | bytes 294920 | tf_op jit(solution)/shard_map/ppermute | solution.py:331
  70.6 7.6 %collective-permute-start.18 = (bf16[1,192,256]{2,1,0:T(8,128)(2,1)S(1)}, bf16[1,192,256]{2,1,0:T(8,128)(2,1)S(1)}, u32[]{:S(2)}, u32[]{:S(2)}) collective-permute-start(bf16[1,192,256]{2,1,0:T(8,128)(2,1)S(1)} %get-tuple-element.84), channel_id=1, source_target_pairs={{0,12},{2,14},{4,8},{6,10},{8,4},{10,6},{12,0},{14,2},{1,13},{3,15... | collective-permute-start | bytes 294920 | tf_op jit(solution)/shard_map/ppermute | solution.py:331
  72.1 8.3 %collective-permute-start.19 = (bf16[1,192,256]{2,1,0:T(8,128)(2,1)S(1)}, bf16[1,192,256]{2,1,0:T(8,128)(2,1)S(1)}, u32[]{:S(2)}, u32[]{:S(2)}) collective-permute-start(bf16[1,192,256]{2,1,0:T(8,128)(2,1)S(1)} %get-tuple-element.75), channel_id=1, source_target_pairs={{0,14},{2,12},{4,10},{6,8},{8,6},{10,4},{12,2},{14,0},{1,15},{3,13... | collective-permute-start | bytes 294920 | tf_op jit(solution)/shard_map/ppermute | solution.py:331
  76.2 5.0 %collective-permute-start.14 = (bf16[1,192,256]{2,1,0:T(8,128)(2,1)S(1)}, bf16[1,192,256]{2,1,0:T(8,128)(2,1)S(1)}, u32[]{:S(2)}, u32[]{:S(2)}) collective-permute-start(bf16[1,192,256]{2,1,0:T(8,128)(2,1)S(1)} %get-tuple-element.80), channel_id=1, source_target_pairs={{0,2},{2,0},{4,6},{6,4},{8,10},{10,8},{12,14},{14,12},{1,3},{3,1},... | collective-permute-start | bytes 294920 | tf_op jit(solution)/shard_map/ppermute | solution.py:331
  76.3 6.9 %collective-permute-start.15 = (bf16[1,192,256]{2,1,0:T(8,128)(2,1)S(1)}, bf16[1,192,256]{2,1,0:T(8,128)(2,1)S(1)}, u32[]{:S(2)}, u32[]{:S(2)}) collective-permute-start(bf16[1,192,256]{2,1,0:T(8,128)(2,1)S(1)} %get-tuple-element.81), channel_id=1, source_target_pairs={{0,4},{2,6},{4,0},{6,2},{8,12},{10,14},{12,8},{14,10},{1,5},{3,7},... | collective-permute-start | bytes 294920 | tf_op jit(solution)/shard_map/ppermute | solution.py:331
  76.7 7.5 %collective-permute-start.16 = (bf16[1,192,256]{2,1,0:T(8,128)(2,1)S(1)}, bf16[1,192,256]{2,1,0:T(8,128)(2,1)S(1)}, u32[]{:S(2)}, u32[]{:S(2)}) collective-permute-start(bf16[1,192,256]{2,1,0:T(8,128)(2,1)S(1)} %get-tuple-element.82), channel_id=1, source_target_pairs={{0,6},{2,4},{4,2},{6,0},{8,14},{10,12},{12,10},{14,8},{1,7},{3,5},... | collective-permute-start | bytes 294920 | tf_op jit(solution)/shard_map/ppermute | solution.py:331

commit v2 on v1

--- a/solution.py
+++ b/solution.py
@@ -132,18 +132,22 @@
             total, summed, at = 0.0, 0.0, 0
             for s in parts:
                 w = jnp.exp2(s * exp2_scale - top)
-                total = total + jnp.sum(w, axis=-1, keepdims=True)
-                summed = summed + jnp.dot(
+                val = vals[at : at + s.shape[1], head]
+                both = jnp.dot(
                     w.astype(jnp.bfloat16),
-                    vals[at : at + s.shape[1], head],
+                    jnp.concatenate([val, jnp.ones_like(val)], axis=1),
                     preferred_element_type=jnp.float32,
                 )
+                summed, total = summed + both[:, :HDIM], total + both[:, HDIM:]
                 at += s.shape[1]
             w = jnp.exp2(s_inner * exp2_scale - top[rows:])
-            total_inner = total[rows:] + jnp.sum(w, axis=-1, keepdims=True)
-            summed_inner = summed[rows:] + jnp.dot(
-                w.astype(jnp.bfloat16), vals[inner, head], preferred_element_type=jnp.float32
+            val = vals[inner, head]
+            both = jnp.dot(
+                w.astype(jnp.bfloat16),
+                jnp.concatenate([val, jnp.ones_like(val)], axis=1),
+                preferred_element_type=jnp.float32,
             )
+            summed_inner, total_inner = summed[rows:] + both[:, :HDIM], total[rows:] + both[:, HDIM:]
             if begin:
                 for i, row in (
                     (at_query + base, (summed[:rows], top[:rows], total[:rows])),

time: 86.6 us -> 87.3 us (level); the launches traced: 85.2 us -> 86.9 us
  waiting for transfers between devices: 28.8 us -> 30.9 us
    ppermute x18, waiting for transfers between devices: 28.8 us -> 30.9 us  [send(): return lax.ppermute(x, 'seq', [(i, i ^ k) for i in range(n_seq)])]
where the time goes in v2:
time: 87.3 us; the launch traced here: 86.9 us
  starting transfers between devices  36.7 us (42%)
  waiting for transfers between devices  30.9 us (35%)
  Pallas kernels  13.9 us (16%)
  local copies, waits for them, and re-layouts  4.18 us (5%)
  between operations  1.15 us (1%)
    ppermute x18, starting transfers between devices, send(): return lax.ppermute(x, 'seq', [(i, i ^ k) for i in range(n_seq)])  31.7 us
    ppermute x18, waiting for transfers between devices, send(): return lax.ppermute(x, 'seq', [(i, i ^ k) for i in range(n_seq)])  30.9 us
    pallas_call x3, Pallas kernels, attend(): pl.pallas_call(functools.partial(attend_kernel, flag, turns, begin), in_s...  10.9 us
    ppermute x2, starting transfers between devices, to_halo(): return lax.ppermute(x, ('seq', 'sp'), pairs)  4.98 us
    unnamed x24, local copies, waits for them, and re-layouts  4.18 us
  transfers between devices with their start and end apart: 20, of which 8 were waited for; matrix products, arithmetic and copies ran while one was open for 0% of the time, Pallas kernels for 15%

profile of v2, /device:TPU:0, one launch (start us, length us, event | category | flops | bytes accessed | tf_op | source)
XLA Modules:
  0.0 86.9 jit_solution(15736393792609262457)
XLA Ops:
  0.0 1.1 %copy-done = bf16[1,192,2048]{2,1,0:T(8,128)(2,1)S(1)} copy-done((bf16[1,192,2048]{2,1,0:T(8,128)(2,1)S(1)}, bf16[1,192,2048]{2,1,0:T(8,128)(2,1)}, u32[]{:S(2)}) %copy-start) | copy-done | bytes 786456
  1.1 1.1 %copy-done.1 = bf16[1,192,2048]{2,1,0:T(8,128)(2,1)S(1)} copy-done((bf16[1,192,2048]{2,1,0:T(8,128)(2,1)S(1)}, bf16[1,192,2048]{2,1,0:T(8,128)(2,1)}, u32[]{:S(2)}) %copy-start.1) | copy-done | bytes 786456
  2.3 0.2 shard_map.64
  2.5 0.9 %copy-done.2 = bf16[1,192,2048]{2,1,0:T(8,128)(2,1)S(1)} copy-done((bf16[1,192,2048]{2,1,0:T(8,128)(2,1)S(1)}, bf16[1,192,2048]{2,1,0:T(8,128)(2,1)}, u32[]{:S(2)}) %copy-start.2) | copy-done | bytes 786456
  3.4 0.3 shard_map.65
  3.7 0.5 collective-permute-start
  4.2 2.7 %collective-permute-start.1 = (bf16[3,192,256]{2,1,0:T(8,128)(2,1)S(1)}, bf16[3,192,256]{2,1,0:T(8,128)(2,1)S(1)}, u32[]{:S(2)}, u32[]{:S(2)}) collective-permute-start(bf16[3,192,256]{2,1,0:T(8,128)(2,1)S(1)} %get-tuple-element.54), channel_id=1, source_target_pairs={{0,6},{2,4},{4,2},{6,0},{8,14},{10,12},{12,10},{14,8},{1,7},{3,5},... | collective-permute-start | bytes 884744 | tf_op jit(solution)/shard_map/ppermute | solution.py:335
  6.9 0.0 collective-permute-start.2
  7.0 3.0 %collective-permute-start.3 = (bf16[2,192,256]{2,1,0:T(8,128)(2,1)S(1)}, bf16[2,192,256]{2,1,0:T(8,128)(2,1)S(1)}, u32[]{:S(2)}, u32[]{:S(2)}) collective-permute-start(bf16[2,192,256]{2,1,0:T(8,128)(2,1)S(1)} %get-tuple-element.45), channel_id=1, source_target_pairs={{0,8},{2,10},{4,12},{6,14},{8,0},{10,2},{12,4},{14,6},{1,9},{3,11}... | collective-permute-start | bytes 589832 | tf_op jit(solution)/shard_map/ppermute | solution.py:335
  10.0 3.0 %collective-permute-start.5 = (bf16[2,192,256]{2,1,0:T(8,128)(2,1)S(1)}, bf16[2,192,256]{2,1,0:T(8,128)(2,1)S(1)}, u32[]{:S(2)}, u32[]{:S(2)}) collective-permute-start(bf16[2,192,256]{2,1,0:T(8,128)(2,1)S(1)} %get-tuple-element.56), channel_id=1, source_target_pairs={{0,12},{2,14},{4,8},{6,10},{8,4},{10,6},{12,0},{14,2},{1,13},{3,15... | collective-permute-start | bytes 589832 | tf_op jit(solution)/shard_map/ppermute | solution.py:335
  13.0 0.2 shard_map.66
  13.2 0.0 copy-start.5
  13.2 9.4 %collective-permute-done.1.refs_3_.refs_2_ = bf16[3,192,256]{2,1,0:T(8,128)(2,1)S(1)} collective-permute-done((bf16[3,192,256]{2,1,0:T(8,128)(2,1)S(1)}, bf16[3,192,256]{2,1,0:T(8,128)(2,1)S(1)}, u32[]{:S(2)}, u32[]{:S(2)}) %collective-permute-start.1) | collective-permute-done | bytes 294944 | tf_op jit(solution)/shard_map/ppermute | solution.py:335
  22.6 4.0 %collective-permute-start.6 = (bf16[2,192,256]{2,1,0:T(8,128)(2,1)S(1)}, bf16[2,192,256]{2,1,0:T(8,128)(2,1)S(1)}, u32[]{:S(2)}, u32[]{:S(2)}) collective-permute-start(bf16[2,192,256]{2,1,0:T(8,128)(2,1)S(1)} %get-tuple-element.61), channel_id=1, source_target_pairs={{0,14},{2,12},{4,10},{6,8},{8,6},{10,4},{12,2},{14,0},{1,15},{3,13... | collective-permute-start | bytes 589832 | tf_op jit(solution)/shard_map/ppermute | solution.py:335
  26.6 2.6 %collective-permute-done.2.refs_2_.refs_3_ = bf16[3,192,256]{2,1,0:T(8,128)(2,1)S(1)} collective-permute-done((bf16[3,192,256]{2,1,0:T(8,128)(2,1)S(1)}, bf16[3,192,256]{2,1,0:T(8,128)(2,1)S(1)}, u32[]{:S(2)}, u32[]{:S(2)}) %collective-permute-start.2) | collective-permute-done | bytes 294944 | tf_op jit(solution)/shard_map/ppermute | solution.py:335
  29.2 0.1 shard_map.68.refs_5_.refs_7_.refs_3_
  29.3 0.0 collective-permute-done.3.refs_0_
  29.3 0.0 collective-permute-done.4.refs_1_
  29.4 6.9 %collective-permute-done.5.refs_2_ = bf16[2,192,256]{2,1,0:T(8,128)(2,1)S(1)} collective-permute-done((bf16[2,192,256]{2,1,0:T(8,128)(2,1)S(1)}, bf16[2,192,256]{2,1,0:T(8,128)(2,1)S(1)}, u32[]{:S(2)}, u32[]{:S(2)}) %collective-permute-start.5) | collective-permute-done | bytes 196640 | tf_op jit(solution)/shard_map/ppermute | solution.py:335
  36.3 1.3 %collective-permute-start.11 = (bf16[4,2,192,256]{3,2,1,0:T(8,128)(2,1)S(1)}, bf16[4,2,192,256]{3,2,1,0:T(8,128)(2,1)}, u32[]{:S(2)}, u32[]{:S(2)}) collective-permute-start(bf16[4,2,192,256]{3,2,1,0:T(8,128)(2,1)S(1)} %shard_map.68.refs_5_.refs_7_.refs_3_), channel_id=1, source_target_pairs={{8,9},{10,11},{12,13},{14,15},{1,0},{3,2},{5,4},{7,6},{24,25},{26,... | collective-permute-start | bytes 2359304 | tf_op jit(solution)/shard_map/ppermute | solution.py:341
  37.6 1.8 %collective-permute-done.6.refs_3_ = bf16[2,192,256]{2,1,0:T(8,128)(2,1)S(1)} collective-permute-done((bf16[2,192,256]{2,1,0:T(8,128)(2,1)S(1)}, bf16[2,192,256]{2,1,0:T(8,128)(2,1)S(1)}, u32[]{:S(2)}, u32[]{:S(2)}) %collective-permute-start.6) | collective-permute-done | bytes 196640 | tf_op jit(solution)/shard_map/ppermute | solution.py:335
  39.3 0.1 shard_map.67.refs_6_.refs_4_
  39.4 3.7 %collective-permute-start.7 = (bf16[4,2,192,256]{3,2,1,0:T(8,128)(2,1)S(1)}, bf16[4,2,192,256]{3,2,1,0:T(8,128)(2,1)S(1)}, u32[]{:S(2)}, u32[]{:S(2)}) collective-permute-start(bf16[4,2,192,256]{3,2,1,0:T(8,128)(2,1)S(1)} %shard_map.67.refs_6_.refs_4_), channel_id=1, source_target_pairs={{0,1},{2,3},{4,5},{6,7},{9,8},{11,10},{13,12},{15,14},{16,17},{18,... | collective-permute-start | bytes 2359304 | tf_op jit(solution)/shard_map/ppermute | solution.py:341
  43.8 0.1 pad_add_fusion.info
  43.9 4.8 %collective-permute-start.10 = (bf16[1,192,256]{2,1,0:T(8,128)(2,1)}, bf16[1,192,256]{2,1,0:T(8,128)(2,1)S(1)}, u32[]{:S(2)}, u32[]{:S(2)}) collective-permute-start(bf16[1,192,256]{2,1,0:T(8,128)(2,1)} %copy-done.10), channel_id=1, source_target_pairs={{0,10},{2,8},{4,14},{6,12},{8,2},{10,0},{12,6},{14,4},{1,11},{3,9}... | collective-permute-start | bytes 294920 | tf_op jit(solution)/shard_map/ppermute | solution.py:335
  48.7 1.9 %collective-permute-start.9 = (bf16[1,192,256]{2,1,0:T(8,128)(2,1)}, bf16[1,192,256]{2,1,0:T(8,128)(2,1)S(1)}, u32[]{:S(2)}, u32[]{:S(2)}) collective-permute-start(bf16[1,192,256]{2,1,0:T(8,128)(2,1)} %copy-done.11), channel_id=1, source_target_pairs={{0,8},{2,10},{4,12},{6,14},{8,0},{10,2},{12,4},{14,6},{1,9},{3,11}... | collective-permute-start | bytes 294920 | tf_op jit(solution)/shard_map/ppermute | solution.py:335
  50.6 1.3 %collective-permute-start.8 = (bf16[1,192,256]{2,1,0:T(8,128)(2,1)}, bf16[1,192,256]{2,1,0:T(8,128)(2,1)S(1)}, u32[]{:S(2)}, u32[]{:S(2)}) collective-permute-start(bf16[1,192,256]{2,1,0:T(8,128)(2,1)} %copy-done.9), channel_id=1, source_target_pairs={{0,14},{2,12},{4,10},{6,8},{8,6},{10,4},{12,2},{14,0},{1,15},{3,13... | collective-permute-start | bytes 294920 | tf_op jit(solution)/shard_map/ppermute | solution.py:335
  51.9 0.9 %copy-done.6 = bf16[2,256,256]{2,1,0:T(8,128)(2,1)S(1)} copy-done((bf16[2,256,256]{2,1,0:T(8,128)(2,1)S(1)}, bf16[2,256,256]{2,1,0:T(8,128)(2,1)}, u32[]{:S(2)}) %copy-start.6) | copy-done | bytes 262168
  52.8 4.3 %shard_map.69 = (f32[4,192,256]{2,1,0:T(8,128)S(1)}, f32[4,192,256]{2,1,0:T(8,128)S(1)}, f32[4,192,256]{2,1,0:T(8,128)S(1)}) custom-call(s32[4]{0:T(128)S(1)} %pad_add_fusion.info, bf16[3,192,256]{2,1,0:T(8,128)(2,1)S(1)} %get-tuple-element.52.refs_0_, bf16[3,192,256]{2,1,0:T(8,128)(2,1)S(1)} %collective-permute-done.refs_1_, ...), custom_call_target="tpu_custom_call" | custom-call | flops 1560281088 | bytes 2818048 | tf_op jit(solution)/shard_map/pallas_call | solution.py:270
  57.2 0.0 collective-permute-done.11.refs_5_
  57.2 2.2 %collective-permute-start.12 = (bf16[1,192,256]{2,1,0:T(8,128)(2,1)S(1)}, bf16[1,192,256]{2,1,0:T(8,128)(2,1)S(1)}, u32[]{:S(2)}, u32[]{:S(2)}) collective-permute-start(bf16[1,192,256]{2,1,0:T(8,128)(2,1)S(1)} %copy-done.8), channel_id=1, source_target_pairs={{0,12},{2,14},{4,8},{6,10},{8,4},{10,6},{12,0},{14,2},{1,13},{3,15... | collective-permute-start | bytes 294920 | tf_op jit(solution)/shard_map/ppermute | solution.py:335
  59.4 4.9 %collective-permute-done.9.refs_0_ = bf16[1,192,256]{2,1,0:T(8,128)(2,1)S(1)} collective-permute-done((bf16[1,192,256]{2,1,0:T(8,128)(2,1)}, bf16[1,192,256]{2,1,0:T(8,128)(2,1)S(1)}, u32[]{:S(2)}, u32[]{:S(2)}) %collective-permute-start.9) | collective-permute-done | bytes 98336 | tf_op jit(solution)/shard_map/ppermute | solution.py:335
  64.4 3.2 %shard_map.70 = (bf16[1,192,256]{2,1,0:T(8,128)(2,1)S(1)}, bf16[1,192,256]{2,1,0:T(8,128)(2,1)S(1)}) custom-call(s32[4]{0:T(128)S(1)} %pad_add_fusion.info, bf16[1,192,256]{2,1,0:T(8,128)(2,1)S(1)} %collective-permute-done.9.refs_0_, bf16[1,192,256]{2,1,0:T(8,128)(2,1)S(1)} %collective-permute-done.10.refs_1_, bf16[2,256,256]{2,1,0:T(8,128)(2,1)S(1)} %copy-done.6, ...), custom_call_target="tpu_custom_call" | custom-call | flops 780140544 | bytes 2424832 | tf_op jit(solution)/shard_map/pallas_call | solution.py:270
  67.6 0.1 collective-permute-start.13
  67.7 0.1 collective-permute-start.17
  67.7 0.0 collective-permute-done.12.refs_1_
  67.7 3.4 %shard_map.71 = (bf16[1,192,256]{2,1,0:T(8,128)(2,1)S(1)}, bf16[1,192,256]{2,1,0:T(8,128)(2,1)S(1)}) custom-call(s32[4]{0:T(128)S(1)} %pad_add_fusion.info, bf16[1,192,256]{2,1,0:T(8,128)(2,1)S(1)} %collective-permute-done.8.refs_0_, bf16[1,192,256]{2,1,0:T(8,128)(2,1)S(1)} %collective-permute-done.12.refs_1_, bf16[2,256,256]{2,1,0:T(8,128)(2,1)S(1)} %copy-done.6, ...), custom_call_target="tpu_custom_call" | custom-call | flops 780140544 | bytes 2424832 | tf_op jit(solution)/shard_map/pallas_call | solution.py:270
  71.1 1.0 %collective-permute-start.18 = (bf16[1,192,256]{2,1,0:T(8,128)(2,1)S(1)}, bf16[1,192,256]{2,1,0:T(8,128)(2,1)S(1)}, u32[]{:S(2)}, u32[]{:S(2)}) collective-permute-start(bf16[1,192,256]{2,1,0:T(8,128)(2,1)S(1)} %get-tuple-element.84), channel_id=1, source_target_pairs={{0,12},{2,14},{4,8},{6,10},{8,4},{10,6},{12,0},{14,2},{1,13},{3,15... | collective-permute-start | bytes 294920 | tf_op jit(solution)/shard_map/ppermute | solution.py:335
  72.1 5.1 %collective-permute-start.19 = (bf16[1,192,256]{2,1,0:T(8,128)(2,1)S(1)}, bf16[1,192,256]{2,1,0:T(8,128)(2,1)S(1)}, u32[]{:S(2)}, u32[]{:S(2)}) collective-permute-start(bf16[1,192,256]{2,1,0:T(8,128)(2,1)S(1)} %get-tuple-element.75), channel_id=1, source_target_pairs={{0,14},{2,12},{4,10},{6,8},{8,6},{10,4},{12,2},{14,0},{1,15},{3,13... | collective-permute-start | bytes 294920 | tf_op jit(solution)/shard_map/ppermute | solution.py:335
  77.3 0.7 shard_map.72
  78.0 0.1 collective-permute-start.14
  78.1 0.1 collective-permute-start.15
  78.1 1.8 %collective-permute-start.16 = (bf16[1,192,256]{2,1,0:T(8,128)(2,1)S(1)}, bf16[1,192,256]{2,1,0:T(8,128)(2,1)S(1)}, u32[]{:S(2)}, u32[]{:S(2)}) collective-permute-start(bf16[1,192,256]{2,1,0:T(8,128)(2,1)S(1)} %get-tuple-element.82), channel_id=1, source_target_pairs={{0,6},{2,4},{4,2},{6,0},{8,14},{10,12},{12,10},{14,8},{1,7},{3,5},... | collective-permute-start | bytes 294920 | tf_op jit(solution)/shard_map/ppermute | solution.py:335
  79.9 1.9 %collective-permute-done.19.refs_3_ = bf16[1,192,256]{2,1,0:T(8,128)(2,1)S(1)} collective-permute-done((bf16[1,192,256]{2,1,0:T(8,128)(2,1)S(1)}, bf16[1,192,256]{2,1,0:T(8,128)(2,1)S(1)}, u32[]{:S(2)}, u32[]{:S(2)}) %collective-permute-start.19) | collective-permute-done | bytes 98336 | tf_op jit(solution)/shard_map/ppermute | solution.py:335
  81.8 0.8 shard_map.73.refs_4_
  82.6 1.3 %collective-permute-done.15.refs_2_ = bf16[1,192,256]{2,1,0:T(8,128)(2,1)S(1)} collective-permute-done((bf16[1,192,256]{2,1,0:T(8,128)(2,1)S(1)}, bf16[1,192,256]{2,1,0:T(8,128)(2,1)S(1)}, u32[]{:S(2)}, u32[]{:S(2)}) %collective-permute-start.15) | collective-permute-done | bytes 98336 | tf_op jit(solution)/shard_map/ppermute | solution.py:335
  83.9 2.0 %collective-permute-done.16.refs_3_ = bf16[1,192,256]{2,1,0:T(8,128)(2,1)S(1)} collective-permute-done((bf16[1,192,256]{2,1,0:T(8,128)(2,1)S(1)}, bf16[1,192,256]{2,1,0:T(8,128)(2,1)S(1)}, u32[]{:S(2)}, u32[]{:S(2)}) %collective-permute-start.16) | collective-permute-done | bytes 98336 | tf_op jit(solution)/shard_map/ppermute | solution.py:335
  85.9 0.8 shard_map.74
  (28 shorter events, 0.1 us)
Async XLA Ops:
  0.0 1.1 %copy-start = (bf16[1,192,2048]{2,1,0:T(8,128)(2,1)S(1)}, bf16[1,192,2048]{2,1,0:T(8,128)(2,1)}, u32[]{:S(2)}) copy-start(bf16[1,192,2048]{2,1,0:T(8,128)(2,1)} %refs_0_.2) | copy-start | bytes 2359300
  1.1 1.1 %copy-start.1 = (bf16[1,192,2048]{2,1,0:T(8,128)(2,1)S(1)}, bf16[1,192,2048]{2,1,0:T(8,128)(2,1)}, u32[]{:S(2)}) copy-start(bf16[1,192,2048]{2,1,0:T(8,128)(2,1)} %refs_1_.2) | copy-start | bytes 2359300
  2.3 1.1 %copy-start.2 = (bf16[1,192,2048]{2,1,0:T(8,128)(2,1)S(1)}, bf16[1,192,2048]{2,1,0:T(8,128)(2,1)}, u32[]{:S(2)}) copy-start(bf16[1,192,2048]{2,1,0:T(8,128)(2,1)} %refs_0_.3) | copy-start | bytes 2359300
  3.4 9.6 %copy-start.3 = (bf16[256,2048]{1,0:T(8,128)(2,1)S(1)}, bf16[256,2048]{1,0:T(8,128)(2,1)}, u32[]{:S(2)}) copy-start(bf16[256,2048]{1,0:T(8,128)(2,1)} %param.9) | copy-start | bytes 3145732
  3.4 9.6 %copy-start.4 = (bf16[256,2048]{1,0:T(8,128)(2,1)S(1)}, bf16[256,2048]{1,0:T(8,128)(2,1)}, u32[]{:S(2)}) copy-start(bf16[256,2048]{1,0:T(8,128)(2,1)} %param.10) | copy-start | bytes 3145732
  3.7 6.3 %collective-permute-start = (bf16[3,192,256]{2,1,0:T(8,128)(2,1)S(1)}, bf16[3,192,256]{2,1,0:T(8,128)(2,1)S(1)}, u32[]{:S(2)}, u32[]{:S(2)}) collective-permute-start(bf16[3,192,256]{2,1,0:T(8,128)(2,1)S(1)} %get-tuple-element.53), channel_id=1, source_target_pairs={{0,2},{2,0},{4,6},{6,4},{8,10},{10,8},{12,14},{14,12},{1,3},{3,1},... | collective-permute-start | bytes 884744 | tf_op jit(solution)/shard_map/ppermute | solution.py:335
  4.2 18.4 %collective-permute-start.1 = (bf16[3,192,256]{2,1,0:T(8,128)(2,1)S(1)}, bf16[3,192,256]{2,1,0:T(8,128)(2,1)S(1)}, u32[]{:S(2)}, u32[]{:S(2)}) collective-permute-start(bf16[3,192,256]{2,1,0:T(8,128)(2,1)S(1)} %get-tuple-element.54), channel_id=1, source_target_pairs={{0,6},{2,4},{4,2},{6,0},{8,14},{10,12},{12,10},{14,8},{1,7},{3,5},... | collective-permute-start | bytes 884744 | tf_op jit(solution)/shard_map/ppermute | solution.py:335
  6.9 22.3 %collective-permute-start.2 = (bf16[3,192,256]{2,1,0:T(8,128)(2,1)S(1)}, bf16[3,192,256]{2,1,0:T(8,128)(2,1)S(1)}, u32[]{:S(2)}, u32[]{:S(2)}) collective-permute-start(bf16[3,192,256]{2,1,0:T(8,128)(2,1)S(1)} %get-tuple-element.55), channel_id=1, source_target_pairs={{0,4},{2,6},{4,0},{6,2},{8,12},{10,14},{12,8},{14,10},{1,5},{3,7},... | collective-permute-start | bytes 884744 | tf_op jit(solution)/shard_map/ppermute | solution.py:335
  7.0 22.4 %collective-permute-start.3 = (bf16[2,192,256]{2,1,0:T(8,128)(2,1)S(1)}, bf16[2,192,256]{2,1,0:T(8,128)(2,1)S(1)}, u32[]{:S(2)}, u32[]{:S(2)}) collective-permute-start(bf16[2,192,256]{2,1,0:T(8,128)(2,1)S(1)} %get-tuple-element.45), channel_id=1, source_target_pairs={{0,8},{2,10},{4,12},{6,14},{8,0},{10,2},{12,4},{14,6},{1,9},{3,11}... | collective-permute-start | bytes 589832 | tf_op jit(solution)/shard_map/ppermute | solution.py:335
  10.0 19.4 %collective-permute-start.4 = (bf16[2,192,256]{2,1,0:T(8,128)(2,1)S(1)}, bf16[2,192,256]{2,1,0:T(8,128)(2,1)S(1)}, u32[]{:S(2)}, u32[]{:S(2)}) collective-permute-start(bf16[2,192,256]{2,1,0:T(8,128)(2,1)S(1)} %get-tuple-element.46), channel_id=1, source_target_pairs={{0,10},{2,8},{4,14},{6,12},{8,2},{10,0},{12,6},{14,4},{1,11},{3,9}... | collective-permute-start | bytes 589832 | tf_op jit(solution)/shard_map/ppermute | solution.py:335
  10.0 26.3 %collective-permute-start.5 = (bf16[2,192,256]{2,1,0:T(8,128)(2,1)S(1)}, bf16[2,192,256]{2,1,0:T(8,128)(2,1)S(1)}, u32[]{:S(2)}, u32[]{:S(2)}) collective-permute-start(bf16[2,192,256]{2,1,0:T(8,128)(2,1)S(1)} %get-tuple-element.56), channel_id=1, source_target_pairs={{0,12},{2,14},{4,8},{6,10},{8,4},{10,6},{12,0},{14,2},{1,13},{3,15... | collective-permute-start | bytes 589832 | tf_op jit(solution)/shard_map/ppermute | solution.py:335
  13.2 16.1 %copy-start.5 = (bf16[2,256,256]{2,1,0:T(8,128)(2,1)}, bf16[2,256,256]{2,1,0:T(8,128)(2,1)S(1)}, u32[]{:S(2)}) copy-start(bf16[2,256,256]{2,1,0:T(8,128)(2,1)S(1)} %get-tuple-element.60.refs_4_.refs_2_) | copy-start | bytes 786436
  13.2 16.1 %copy-start.7 = (bf16[1,192,256]{2,1,0:T(8,128)(2,1)}, bf16[1,192,256]{2,1,0:T(8,128)(2,1)S(1)}, u32[]{:S(2)}) copy-start(bf16[1,192,256]{2,1,0:T(8,128)(2,1)S(1)} %get-tuple-element.74) | copy-start | bytes 294916
  13.2 16.1 %copy-start.9 = (bf16[1,192,256]{2,1,0:T(8,128)(2,1)}, bf16[1,192,256]{2,1,0:T(8,128)(2,1)S(1)}, u32[]{:S(2)}) copy-start(bf16[1,192,256]{2,1,0:T(8,128)(2,1)S(1)} %get-tuple-element.63) | copy-start | bytes 294916
  13.2 16.1 %copy-start.10 = (bf16[1,192,256]{2,1,0:T(8,128)(2,1)}, bf16[1,192,256]{2,1,0:T(8,128)(2,1)S(1)}, u32[]{:S(2)}) copy-start(bf16[1,192,256]{2,1,0:T(8,128)(2,1)S(1)} %get-tuple-element.69) | copy-start | bytes 294916
  13.2 16.1 %copy-start.11 = (bf16[1,192,256]{2,1,0:T(8,128)(2,1)}, bf16[1,192,256]{2,1,0:T(8,128)(2,1)S(1)}, u32[]{:S(2)}) copy-start(bf16[1,192,256]{2,1,0:T(8,128)(2,1)S(1)} %get-tuple-element.65) | copy-start | bytes 294916
  22.6 16.7 %collective-permute-start.6 = (bf16[2,192,256]{2,1,0:T(8,128)(2,1)S(1)}, bf16[2,192,256]{2,1,0:T(8,128)(2,1)S(1)}, u32[]{:S(2)}, u32[]{:S(2)}) collective-permute-start(bf16[2,192,256]{2,1,0:T(8,128)(2,1)S(1)} %get-tuple-element.61), channel_id=1, source_target_pairs={{0,14},{2,12},{4,10},{6,8},{8,6},{10,4},{12,2},{14,0},{1,15},{3,13... | collective-permute-start | bytes 589832 | tf_op jit(solution)/shard_map/ppermute | solution.py:335
  36.3 20.9 %collective-permute-start.11 = (bf16[4,2,192,256]{3,2,1,0:T(8,128)(2,1)S(1)}, bf16[4,2,192,256]{3,2,1,0:T(8,128)(2,1)}, u32[]{:S(2)}, u32[]{:S(2)}) collective-permute-start(bf16[4,2,192,256]{3,2,1,0:T(8,128)(2,1)S(1)} %shard_map.68.refs_5_.refs_7_.refs_3_), channel_id=1, source_target_pairs={{8,9},{10,11},{12,13},{14,15},{1,0},{3,2},{5,4},{7,6},{24,25},{26,... | collective-permute-start | bytes 2359304 | tf_op jit(solution)/shard_map/ppermute | solution.py:341
  39.4 37.9 %collective-permute-start.7 = (bf16[4,2,192,256]{3,2,1,0:T(8,128)(2,1)S(1)}, bf16[4,2,192,256]{3,2,1,0:T(8,128)(2,1)S(1)}, u32[]{:S(2)}, u32[]{:S(2)}) collective-permute-start(bf16[4,2,192,256]{3,2,1,0:T(8,128)(2,1)S(1)} %shard_map.67.refs_6_.refs_4_), channel_id=1, source_target_pairs={{0,1},{2,3},{4,5},{6,7},{9,8},{11,10},{13,12},{15,14},{16,17},{18,... | collective-permute-start | bytes 2359304 | tf_op jit(solution)/shard_map/ppermute | solution.py:341
  43.9 20.5 %collective-permute-start.10 = (bf16[1,192,256]{2,1,0:T(8,128)(2,1)}, bf16[1,192,256]{2,1,0:T(8,128)(2,1)S(1)}, u32[]{:S(2)}, u32[]{:S(2)}) collective-permute-start(bf16[1,192,256]{2,1,0:T(8,128)(2,1)} %copy-done.10), channel_id=1, source_target_pairs={{0,10},{2,8},{4,14},{6,12},{8,2},{10,0},{12,6},{14,4},{1,11},{3,9}... | collective-permute-start | bytes 294920 | tf_op jit(solution)/shard_map/ppermute | solution.py:335
  48.7 15.7 %collective-permute-start.9 = (bf16[1,192,256]{2,1,0:T(8,128)(2,1)}, bf16[1,192,256]{2,1,0:T(8,128)(2,1)S(1)}, u32[]{:S(2)}, u32[]{:S(2)}) collective-permute-start(bf16[1,192,256]{2,1,0:T(8,128)(2,1)} %copy-done.11), channel_id=1, source_target_pairs={{0,8},{2,10},{4,12},{6,14},{8,0},{10,2},{12,4},{14,6},{1,9},{3,11}... | collective-permute-start | bytes 294920 | tf_op jit(solution)/shard_map/ppermute | solution.py:335
  50.6 17.1 %collective-permute-start.8 = (bf16[1,192,256]{2,1,0:T(8,128)(2,1)}, bf16[1,192,256]{2,1,0:T(8,128)(2,1)S(1)}, u32[]{:S(2)}, u32[]{:S(2)}) collective-permute-start(bf16[1,192,256]{2,1,0:T(8,128)(2,1)} %copy-done.9), channel_id=1, source_target_pairs={{0,14},{2,12},{4,10},{6,8},{8,6},{10,4},{12,2},{14,0},{1,15},{3,13... | collective-permute-start | bytes 294920 | tf_op jit(solution)/shard_map/ppermute | solution.py:335
  51.9 0.9 %copy-start.6 = (bf16[2,256,256]{2,1,0:T(8,128)(2,1)S(1)}, bf16[2,256,256]{2,1,0:T(8,128)(2,1)}, u32[]{:S(2)}) copy-start(bf16[2,256,256]{2,1,0:T(8,128)(2,1)} %copy-done.5) | copy-start | bytes 786436
  52.8 4.4 %copy-start.8 = (bf16[1,192,256]{2,1,0:T(8,128)(2,1)S(1)}, bf16[1,192,256]{2,1,0:T(8,128)(2,1)}, u32[]{:S(2)}) copy-start(bf16[1,192,256]{2,1,0:T(8,128)(2,1)} %copy-done.7) | copy-start | bytes 294916
  57.2 10.6 %collective-permute-start.12 = (bf16[1,192,256]{2,1,0:T(8,128)(2,1)S(1)}, bf16[1,192,256]{2,1,0:T(8,128)(2,1)S(1)}, u32[]{:S(2)}, u32[]{:S(2)}) collective-permute-start(bf16[1,192,256]{2,1,0:T(8,128)(2,1)S(1)} %copy-done.8), channel_id=1, source_target_pairs={{0,12},{2,14},{4,8},{6,10},{8,4},{10,6},{12,0},{14,2},{1,13},{3,15... | collective-permute-start | bytes 294920 | tf_op jit(solution)/shard_map/ppermute | solution.py:335
  67.6 9.7 %collective-permute-start.13 = (bf16[1,192,256]{2,1,0:T(8,128)(2,1)S(1)}, bf16[1,192,256]{2,1,0:T(8,128)(2,1)S(1)}, u32[]{:S(2)}, u32[]{:S(2)}) collective-permute-start(bf16[1,192,256]{2,1,0:T(8,128)(2,1)S(1)} %get-tuple-element.71), channel_id=1, source_target_pairs={{0,8},{2,10},{4,12},{6,14},{8,0},{10,2},{12,4},{14,6},{1,9},{3,11}... | collective-permute-start | bytes 294920 | tf_op jit(solution)/shard_map/ppermute | solution.py:335
  67.7 10.5 %collective-permute-start.17 = (bf16[1,192,256]{2,1,0:T(8,128)(2,1)S(1)}, bf16[1,192,256]{2,1,0:T(8,128)(2,1)S(1)}, u32[]{:S(2)}, u32[]{:S(2)}) collective-permute-start(bf16[1,192,256]{2,1,0:T(8,128)(2,1)S(1)} %get-tuple-element.83), channel_id=1, source_target_pairs={{0,10},{2,8},{4,14},{6,12},{8,2},{10,0},{12,6},{14,4},{1,11},{3,9}... | collective-permute-start | bytes 294920 | tf_op jit(solution)/shard_map/ppermute | solution.py:335
  71.1 8.8 %collective-permute-start.18 = (bf16[1,192,256]{2,1,0:T(8,128)(2,1)S(1)}, bf16[1,192,256]{2,1,0:T(8,128)(2,1)S(1)}, u32[]{:S(2)}, u32[]{:S(2)}) collective-permute-start(bf16[1,192,256]{2,1,0:T(8,128)(2,1)S(1)} %get-tuple-element.84), channel_id=1, source_target_pairs={{0,12},{2,14},{4,8},{6,10},{8,4},{10,6},{12,0},{14,2},{1,13},{3,15... | collective-permute-start | bytes 294920 | tf_op jit(solution)/shard_map/ppermute | solution.py:335
  72.1 9.7 %collective-permute-start.19 = (bf16[1,192,256]{2,1,0:T(8,128)(2,1)S(1)}, bf16[1,192,256]{2,1,0:T(8,128)(2,1)S(1)}, u32[]{:S(2)}, u32[]{:S(2)}) collective-permute-start(bf16[1,192,256]{2,1,0:T(8,128)(2,1)S(1)} %get-tuple-element.75), channel_id=1, source_target_pairs={{0,14},{2,12},{4,10},{6,8},{8,6},{10,4},{12,2},{14,0},{1,15},{3,13... | collective-permute-start | bytes 294920 | tf_op jit(solution)/shard_map/ppermute | solution.py:335
  78.0 4.7 %collective-permute-start.14 = (bf16[1,192,256]{2,1,0:T(8,128)(2,1)S(1)}, bf16[1,192,256]{2,1,0:T(8,128)(2,1)S(1)}, u32[]{:S(2)}, u32[]{:S(2)}) collective-permute-start(bf16[1,192,256]{2,1,0:T(8,128)(2,1)S(1)} %get-tuple-element.80), channel_id=1, source_target_pairs={{0,2},{2,0},{4,6},{6,4},{8,10},{10,8},{12,14},{14,12},{1,3},{3,1},... | collective-permute-start | bytes 294920 | tf_op jit(solution)/shard_map/ppermute | solution.py:335
  78.1 5.9 %collective-permute-start.15 = (bf16[1,192,256]{2,1,0:T(8,128)(2,1)S(1)}, bf16[1,192,256]{2,1,0:T(8,128)(2,1)S(1)}, u32[]{:S(2)}, u32[]{:S(2)}) collective-permute-start(bf16[1,192,256]{2,1,0:T(8,128)(2,1)S(1)} %get-tuple-element.81), channel_id=1, source_target_pairs={{0,4},{2,6},{4,0},{6,2},{8,12},{10,14},{12,8},{14,10},{1,5},{3,7},... | collective-permute-start | bytes 294920 | tf_op jit(solution)/shard_map/ppermute | solution.py:335
  78.1 7.8 %collective-permute-start.16 = (bf16[1,192,256]{2,1,0:T(8,128)(2,1)S(1)}, bf16[1,192,256]{2,1,0:T(8,128)(2,1)S(1)}, u32[]{:S(2)}, u32[]{:S(2)}) collective-permute-start(bf16[1,192,256]{2,1,0:T(8,128)(2,1)S(1)} %get-tuple-element.82), channel_id=1, source_target_pairs={{0,6},{2,4},{4,2},{6,0},{8,14},{10,12},{12,10},{14,8},{1,7},{3,5},... | collective-permute-start | bytes 294920 | tf_op jit(solution)/shard_map/ppermute | solution.py:335
